TPU v7x, 256 devices: a whole 4x4x8 slice. The times are simulated.
256 devices in a mesh: tile: 32 (over y_lo, z, core), samp: 8 (over y_hi, x).
Axes of the slice: x: 4, y: 4 (y_hi: 2, y_lo: 2; y = y_hi * 2 + y_lo), z: 8, core: 2. Of those that a mesh axis runs over, the one named last changes fastest.
Arguments:
- bathymetry: float32 [6, 512, 512], P(None, 'tile'), may hold values from 0.5 to 2
- initial_state: float32 [16, 6, 512, 512], P(None, None, 'tile'), may hold values from -6 to 6
- patterns: bfloat16 [4, 6, 512, 512], P(None, None, 'tile'), may hold values from -6 to 6
- pattern_index: int32 [8, 16], P('samp'), may hold values from 0 to 3
- coupling: float32 [16, 16], replicated, may hold values from -1.5 to 1.5
- final_weights: float32 [8, 16, 6, 512, 512], P('samp', None, None, 'tile'), may hold values from -6 to 6
Outputs:
- gradient: float32 [6, 512, 512], P(None, 'tile')
All inputs are finite; a program needn't handle non-finite values.
Results may differ from a plain program's by a relative error of at most 0.0003.
Values sent between devices are 32-bit elements; how exact they have to be, the bound alone decides.
A program may use at most 128 MiB of HBM per device.

v0:
```python
import jax
import jax.numpy as jnp
from jax import lax
from jax.sharding import PartitionSpec as P

STEP_FACTOR = 0.1


def with_halo(cells, sides, width):
    for axis, dim in sides:
        count = lax.axis_size(axis)
        head = lax.slice_in_dim(cells, 0, width, axis=dim)
        tail = lax.slice_in_dim(cells, cells.shape[dim] - width, cells.shape[dim], axis=dim)
        cells = jnp.concatenate(
            [
                lax.ppermute(tail, axis, [(i, (i + 1) % count) for i in range(count)]),
                cells,
                lax.ppermute(head, axis, [((i + 1) % count, i) for i in range(count)]),
            ],
            axis=dim,
        )
    return cells


def from_root(value, axis, source):
    kept = jnp.where(lax.axis_index(axis) == source, value, 0).astype(value.dtype)
    return lax.psum(kept, axis)


def fill_rims(field):
    tile_count = lax.axis_size("tile")
    tile_place = lax.axis_index("tile")
    local_width = field.shape[2]
    panel_cells = field.shape[3]
    last = panel_cells - 1
    beside = with_halo(field, (("tile", 2),), 1)
    edge_stack = jnp.stack(
        [
            field[:, 1, :, last],
            field[:, 1, :, 0],
            field[:, 2, :, last],
            field[:, 2, :, 0],
            field[:, 3, :, last],
            field[:, 3, :, 0],
            field[:, 4, :, last],
            field[:, 5, :, 0],
        ],
        axis=1,
    )
    gathered = lax.all_gather(edge_stack, "tile", axis=2, tiled=True)
    pole_first = from_root(jnp.stack([field[:, 4, 0, :], field[:, 5, 0, :]], axis=1), "tile", 0)
    pole_last = from_root(
        jnp.stack([field[:, 4, local_width - 1, :], field[:, 5, local_width - 1, :]], axis=1),
        "tile",
        tile_count - 1,
    )
    western = beside[:, :, 0, :]
    eastern = beside[:, :, -1, :]
    west_fix = jnp.concatenate(
        [western[:, 3:4], western[:, 0:3], gathered[:, 4:5, ::-1], gathered[:, 5:6]], axis=1
    )
    east_fix = jnp.concatenate(
        [eastern[:, 1:4], eastern[:, 0:1], gathered[:, 0:1], gathered[:, 1:2, ::-1]], axis=1
    )
    western = jnp.where(tile_place == 0, west_fix, western)
    eastern = jnp.where(tile_place == tile_count - 1, east_fix, eastern)
    interior = jnp.concatenate(
        [western[:, :, None], beside[:, :, 1:-1], eastern[:, :, None]], axis=2
    )
    offset = tile_place * local_width
    mirror = (tile_count - 1 - tile_place) * local_width

    def window(line, at):
        return lax.dynamic_slice_in_dim(line, at, local_width, axis=line.ndim - 1)

    def window_back(line):
        return window(line, mirror)[..., ::-1]

    northern = jnp.stack(
        [
            field[:, 4, :, 0],
            window(pole_last[:, 0], offset),
            window_back(gathered[:, 6]),
            window_back(pole_first[:, 0]),
            window_back(gathered[:, 2]),
            field[:, 0, :, 0],
        ],
        axis=1,
    )
    southern = jnp.stack(
        [
            field[:, 5, :, last],
            window_back(pole_last[:, 1]),
            window_back(gathered[:, 7]),
            window(pole_first[:, 1], offset),
            field[:, 0, :, last],
            window_back(gathered[:, 3]),
        ],
        axis=1,
    )
    padding = jnp.zeros(field.shape[:2] + (1,), field.dtype)
    north_line = jnp.concatenate([padding, northern, padding], axis=2)[..., None]
    south_line = jnp.concatenate([padding, southern, padding], axis=2)[..., None]
    return jnp.concatenate([south_line, interior, north_line], axis=3)


def stencil(padded, depth_pad):
    rows_i = padded.shape[-2] - 2
    rows_j = padded.shape[-1] - 2
    centre = padded[..., 1 : 1 + rows_i, 1 : 1 + rows_j]
    depth_here = depth_pad[..., 1 : 1 + rows_i, 1 : 1 + rows_j]
    summed = jnp.zeros_like(centre)
    for shift_i, shift_j in ((1, 0), (-1, 0), (0, 1), (0, -1)):
        beside_value = padded[
            ..., 1 + shift_i : 1 + shift_i + rows_i, 1 + shift_j : 1 + shift_j + rows_j
        ]
        depth_near = depth_pad[
            ..., 1 + shift_i : 1 + shift_i + rows_i, 1 + shift_j : 1 + shift_j + rows_j
        ]
        summed = summed + 0.5 * (depth_here + depth_near) * (beside_value - centre)
    return summed


def edge_term(adjoint_pad, state_pad):
    rows_i = adjoint_pad.shape[-2] - 2
    rows_j = adjoint_pad.shape[-1] - 2
    adjoint_here = adjoint_pad[..., 1 : 1 + rows_i, 1 : 1 + rows_j]
    state_here = state_pad[..., 1 : 1 + rows_i, 1 : 1 + rows_j]
    summed = jnp.zeros_like(adjoint_here)
    for shift_i, shift_j in ((1, 0), (-1, 0), (0, 1), (0, -1)):
        adjoint_near = adjoint_pad[
            ..., 1 + shift_i : 1 + shift_i + rows_i, 1 + shift_j : 1 + shift_j + rows_j
        ]
        state_near = state_pad[
            ..., 1 + shift_i : 1 + shift_i + rows_i, 1 + shift_j : 1 + shift_j + rows_j
        ]
        summed = summed + (adjoint_here - adjoint_near) * (state_near - state_here)
    return 0.5 * jnp.sum(summed, axis=0)


def body(bathymetry, initial_state, patterns, pattern_index, coupling, final_weights):
    layer_count = initial_state.shape[0]
    mixing = jnp.eye(layer_count, dtype=jnp.float32) + coupling
    selector = (
        pattern_index[0][:, None] == jnp.arange(patterns.shape[0], dtype=jnp.int32)[None, :]
    ).astype(jnp.bfloat16)
    forcing = jnp.einsum("lm,mpij->lpij", selector, patterns, preferred_element_type=jnp.float32)
    mixed_zero = jnp.einsum("km,mpij->kpij", mixing, initial_state, precision=lax.Precision.HIGHEST)
    cotangent = final_weights[0]
    depth_pad = fill_rims(bathymetry[None])[0]
    zero_pad = fill_rims(mixed_zero)
    state_one = initial_state + STEP_FACTOR * (stencil(zero_pad, depth_pad) + forcing)
    mixed_one = jnp.einsum("km,mpij->kpij", mixing, state_one, precision=lax.Precision.HIGHEST)
    one_pad = fill_rims(mixed_one)
    weight_pad = fill_rims(cotangent)
    grad_late = STEP_FACTOR * edge_term(weight_pad, one_pad)
    lap_weight = stencil(weight_pad, depth_pad)
    adjoint_one = 2.0 * cotangent + STEP_FACTOR * jnp.einsum(
        "km,kpij->mpij", mixing, lap_weight, precision=lax.Precision.HIGHEST
    )
    adjoint_pad = fill_rims(adjoint_one)
    grad_early = STEP_FACTOR * edge_term(adjoint_pad, zero_pad)
    summed = lax.psum(grad_late + grad_early, "samp")
    return summed / lax.axis_size("samp")


def solution(mesh):
    in_specs = (
        P(None, "tile", None),
        P(None, None, "tile", None),
        P(None, None, "tile", None),
        P("samp", None),
        P(),
        P("samp", None, None, "tile", None),
    )
    out_specs = P(None, "tile", None)
    return jax.shard_map(body, mesh=mesh, in_specs=in_specs, out_specs=out_specs, check_vma=False)
```

profile of v0, /device:TPU:4, one launch (start us, length us, event | category | flops | bytes accessed | tf_op | source)
XLA Modules:
  0.0 998.6 jit_solution(13499920242101245051)
XLA Ops:
  8.2 6.4 collective-permute-start.2
  14.5 6.0 fusion.59
  21.4 3.9 collective-permute-start.3
  37.2 2.8 fusion.122
  42.6 58.2 %all-reduce = (f32[1,2,512]{2,1,0:T(2,128)}, f32[1,2,512]{2,1,0:T(2,128)}) all-reduce(f32[1,2,512]{2,1,0:T(2,128)S(1)} %get-tuple-element.180, f32[1,2,512]{2,1,0:T(2,128)} %get-tuple-element.181), channel_id=1, replica_groups=mesh['tile'=32,'samp'=8] {'tile'}, use_global_device_ids=true, to_apply=%region_0.1 | all-reduce | flops 2048 | bytes 16384 | tf_op jit(solution)/shard_map/psum | solution.py:27
  113.6 31.7 %all_gather.16 = f32[1,8,512]{1,0,2:T(1,128)S(1)} all-gather(f32[1,8,16]{1,0,2:T(1,128)} %copy.1755), channel_id=1, replica_groups=mesh['tile'=32,'samp'=8] {'tile'}, dimensions={2}, use_global_device_ids=true | all-gather | bytes 16896 | tf_op jit(solution)/shard_map/all_gather | solution.py:50
  145.3 6.8 fusion.130
  159.3 2.6 reverse_reduce_fusion
  193.0 38.8 %all_gather.17 = f32[16,8,512]{0,1,2:T(8,128)S(1)} all-gather(f32[16,8,16]{0,1,2:T(8,128)} %copy.1773), channel_id=1, replica_groups=mesh['tile'=32,'samp'=8] {'tile'}, dimensions={2}, use_global_device_ids=true | all-gather | bytes 270336 | tf_op jit(solution)/shard_map/all_gather | solution.py:50
  231.8 2.6 fusion.129
  262.5 37.0 %all_gather.15 = f32[16,8,512]{0,1,2:T(8,128)S(1)} all-gather(f32[16,8,16]{0,1,2:T(8,128)} %copy.1750), channel_id=1, replica_groups=mesh['tile'=32,'samp'=8] {'tile'}, dimensions={2}, use_global_device_ids=true | all-gather | bytes 270336 | tf_op jit(solution)/shard_map/all_gather | solution.py:50
  404.3 2.4 copy.1784
  406.7 10.1 %fusion.48 = f32[16,6,16,512]{3,0,2,1:T(8,128)S(1)} fusion(f32[16,6,16,512]{3,0,2,1:T(8,128)} %fusion.77, f32[16,6,16,512]{3,2,1,0:T(8,128)} %param.7, f32[16,6,16,512]{3,0,2,1:T(8,128)S(1)} %fusion.59, f32[16,6,1,512]{3,0,2,1:T(8,128)S(1)} %fusion.84, f32[16,6,1,512]{3,0,2,1:T(8,128)S(1)} %maximum_select_fusion, f32[6,16,512]{2,1,0:T(8,128)} %get-tuple-element.135, ...), kind=kOutput, calls=%fused_computation.78 | convolution fusion | flops 168297216 | bytes 13777408 | tf_op jit(solution)/shard_map/km,mpij->kpij/dot_general | solution.py:153
  420.2 2.4 copy.1813
  425.0 14.0 %multiply_add_fusion = f32[16,6,16,512]{3,0,2,1:T(8,128)S(1)} fusion(f32[16,6,16,512]{3,0,2,1:T(8,128)} %bitcast.394, f32[16,6,1,512]{3,0,2,1:T(8,128)S(1)} %copy-done.16, f32[16,6,1,512]{3,0,2,1:T(8,128)S(1)} %copy-done.18, f32[16,6,18,1]{3,0,2,1:T(8,128)} %copy.1823, f32[16,6,18,1]{3,0,2,1:T(8,128)} %copy.1813, f32[6,16,512]{2,1,0:T(8,128)} %get-tuple-element.135, ...), kind=kOutput, calls=%fused_computation.77 | convolution fusion | flops 168297216 | bytes 7485952 | tf_op jit(solution)/shard_map/km,kpij->mpij/dot_general | solution.py:158
  442.3 3.9 collective-permute-start.5
  470.1 37.2 %all_gather.18 = f32[16,8,512]{0,1,2:T(8,128)S(1)} all-gather(f32[16,8,16]{0,1,2:T(8,128)S(1)} %copy.1800), channel_id=1, replica_groups=mesh['tile'=32,'samp'=8] {'tile'}, dimensions={2}, use_global_device_ids=true | all-gather | bytes 270336 | tf_op jit(solution)/shard_map/all_gather | solution.py:50
  530.0 2.7 rev.137
  535.6 3.5 collective-permute-start.8
  553.6 36.9 %all_gather.19 = f32[16,8,512]{0,1,2:T(8,128)S(1)} all-gather(f32[16,8,16]{0,1,2:T(8,128)S(1)} %copy.1839), channel_id=1, replica_groups=mesh['tile'=32,'samp'=8] {'tile'}, dimensions={2}, use_global_device_ids=true | all-gather | bytes 270336 | tf_op jit(solution)/shard_map/all_gather | solution.py:50
  625.8 203.2 %all-reduce.9.cloned.1.call-done = (f32[16,2,512]{2,0,1:T(8,128)}, f32[16,2,512]{2,0,1:T(8,128)}, f32[16,2,512]{2,0,1:T(8,128)}, f32[16,2,512]{2,0,1:T(8,128)}) async-done(((f32[16,2,512]{2,0,1:T(8,128)}, f32[16,2,512]{2,0,1:T(8,128)}, f32[16,2,512]{2,0,1:T(8,128)}, f32[16,2,512]{2,0,1:T(8,128)}), (f32[16,2,512]{2,0,1:T(8,128)}, f32[16,2,512]{2,0,1:T(8,128)}, f32[16,2,512]{2,0,1:T(8,128)}, ...) | async-done | bytes 262160 | tf_op jit(solution)/shard_map/psum | solution.py:27
  878.7 18.7 %fusion.15 = f32[6,16,512]{2,1,0:T(8,128)S(1)} fusion(f32[16,6,16,512]{3,0,2,1:T(8,128)} %copy-done.3, f32[16,6,18,1]{3,0,2,1:T(8,128)} %copy.1828, f32[16,6,1,512]{3,0,2,1:T(8,128)} %fusion.85, f32[16,6,1,512]{3,0,2,1:T(8,128)} %maximum_select_fusion.2, f32[16,6,16,512]{3,0,2,1:T(8,128)} %bitcast.395, f32[16,6,1,512]{3,0,2,1:T(8,128)S(1)} %copy-done.17, ...), kind=kLoop, calls=%fused_computation.24 | loop fusion | flops 25116672 | bytes 7302144 | tf_op jit(solution)/shard_map/reduce_sum | solution.py:138
  897.5 6.9 fusion.3
  905.2 84.9 %all-reduce.7.cloned.1.call-done = f32[6,16,512]{2,1,0:T(8,128)} async-done(((f32[6,16,512]{2,1,0:T(8,128)}), f32[6,16,512]{2,1,0:T(8,128)}) %all-reduce.7.cloned.1.call-update) | async-done | bytes 196624 | tf_op jit(solution)/shard_map/psum | solution.py:163
  (413 shorter events, 360.9 us)
Async XLA Ops:
  6.5 297.9 %copy-start = (bf16[4,6,16,512]{3,2,1,0:T(8,128)(2,1)S(1)}, bf16[4,6,16,512]{3,2,1,0:T(8,128)(2,1)}, u32[]{:S(2)}) copy-start(bf16[4,6,16,512]{3,2,1,0:T(8,128)(2,1)} %param.8) | copy-start | bytes 1179652
  6.5 354.6 %all-reduce.11.cloned.1.call-start = ((), (), s32[]{:S(2)}) async-start(), calls=%async_computation.2 | async-start | bytes 524288 | tf_op jit(solution)/shard_map/psum | solution.py:27
  8.2 336.5 %collective-permute-start.1 = (f32[1,6,1,512]{3,2,1,0:T(1,128)}, f32[1,6,1,512]{3,2,1,0:T(1,128)S(1)}, u32[]{:S(2)}, u32[]{:S(2)}) collective-permute-start(f32[1,6,1,512]{3,2,1,0:T(1,128)} %get-tuple-element.144), channel_id=1, source_target_pairs={{0,8},{8,16},{16,24},{24,32},{32,40},{40,48},{48,56},{56,64},{64,7... | collective-permute-start | bytes 36872 | tf_op jit(solution)/shard_map/ppermute | solution.py:16
  8.2 338.5 %collective-permute-start.2 = (f32[1,6,1,512]{3,2,1,0:T(1,128)}, f32[1,6,1,512]{3,2,1,0:T(1,128)}, u32[]{:S(2)}, u32[]{:S(2)}) collective-permute-start(f32[1,6,1,512]{3,2,1,0:T(1,128)} %get-tuple-element.145), channel_id=1, source_target_pairs={{8,0},{16,8},{24,16},{32,24},{40,32},{48,40},{56,48},{64,56},{72,6... | collective-permute-start | bytes 36872 | tf_op jit(solution)/shard_map/ppermute | solution.py:18
  21.4 329.9 %collective-permute-start.4 = (f32[16,6,1,512]{3,0,2,1:T(8,128)}, f32[16,6,1,512]{3,0,2,1:T(8,128)}, u32[]{:S(2)}, u32[]{:S(2)}) collective-permute-start(f32[16,6,1,512]{3,0,2,1:T(8,128)} %get-tuple-element.98), channel_id=1, source_target_pairs={{0,8},{8,16},{16,24},{24,32},{32,40},{40,48},{48,56},{56,64},{64,7... | collective-permute-start | bytes 589832 | tf_op jit(solution)/shard_map/ppermute | solution.py:16
  21.4 331.5 %collective-permute-start.3 = (f32[16,6,1,512]{3,0,2,1:T(8,128)}, f32[16,6,1,512]{3,0,2,1:T(8,128)}, u32[]{:S(2)}, u32[]{:S(2)}) collective-permute-start(f32[16,6,1,512]{3,0,2,1:T(8,128)} %get-tuple-element.99), channel_id=1, source_target_pairs={{8,0},{16,8},{24,16},{32,24},{40,32},{48,40},{56,48},{64,56},{72,6... | collective-permute-start | bytes 589832 | tf_op jit(solution)/shard_map/ppermute | solution.py:18
  27.9 326.7 %collective-permute-start.6 = (f32[16,6,1,512]{3,0,2,1:T(8,128)}, f32[16,6,1,512]{3,0,2,1:T(8,128)}, u32[]{:S(2)}, u32[]{:S(2)}) collective-permute-start(f32[16,6,1,512]{3,0,2,1:T(8,128)} %get-tuple-element.72), channel_id=1, source_target_pairs={{0,8},{8,16},{16,24},{24,32},{32,40},{40,48},{48,56},{56,64},{64,7... | collective-permute-start | bytes 589832 | tf_op jit(solution)/shard_map/ppermute | solution.py:16
  32.5 796.5 %all-reduce.9.cloned.1.call-start = ((), (), s32[]{:S(2)}) async-start(), calls=%async_computation.1 | async-start | bytes 524288 | tf_op jit(solution)/shard_map/psum | solution.py:27
  262.5 41.9 %copy-start.36 = (s32[1,16]{1,0:T(1,128)S(1)}, s32[1,16]{1,0:T(1,128)}, u32[]{:S(2)}) copy-start(s32[1,16]{1,0:T(1,128)} %param.9) | copy-start | bytes 196
  306.7 41.3 %copy-start.34 = (f32[512]{0:T(512)S(1)}, f32[512]{0:T(512)}, u32[]{:S(2)}) copy-start(f32[512]{0:T(512)} %get-tuple-element.140) | copy-start | bytes 6148
  306.7 41.3 %copy-start.35 = (f32[512]{0:T(512)S(1)}, f32[512]{0:T(512)}, u32[]{:S(2)}) copy-start(f32[512]{0:T(512)} %reverse_reduce_fusion) | copy-start | bytes 6148
  344.6 9.9 collective-permute-start
  350.1 36.5 %copy-start.31 = (f32[16,1,16,1]{2,0,3,1:T(8,128)S(1)}, f32[16,1,16,1]{2,0,3,1:T(8,128)}, u32[]{:S(2)}) copy-start(f32[16,1,16,1]{2,0,3,1:T(8,128)} %copy.1868) | copy-start | bytes 3076
  350.1 47.6 %copy-start.32 = (f32[16,1,16,1]{2,0,3,1:T(8,128)S(1)}, f32[16,1,16,1]{2,0,3,1:T(8,128)}, u32[]{:S(2)}) copy-start(f32[16,1,16,1]{2,0,3,1:T(8,128)} %copy.1821) | copy-start | bytes 3076
  356.5 60.3 %copy-start.12 = (f32[16,6,1,512]{3,0,2,1:T(8,128)}, f32[16,6,1,512]{3,0,2,1:T(8,128)S(1)}, u32[]{:S(2)}) copy-start(f32[16,6,1,512]{3,0,2,1:T(8,128)S(1)} %fusion.84) | copy-start | bytes 589828
  357.4 59.4 %copy-start.14 = (f32[16,6,1,512]{3,0,2,1:T(8,128)}, f32[16,6,1,512]{3,0,2,1:T(8,128)S(1)}, u32[]{:S(2)}) copy-start(f32[16,6,1,512]{3,0,2,1:T(8,128)S(1)} %maximum_select_fusion) | copy-start | bytes 589828
  442.2 170.5 %collective-permute-start.7 = (f32[16,6,1,512]{3,0,2,1:T(8,128)}, f32[16,6,1,512]{3,0,2,1:T(8,128)}, u32[]{:S(2)}, u32[]{:S(2)}) collective-permute-start(f32[16,6,1,512]{3,0,2,1:T(8,128)} %get-tuple-element.55), channel_id=1, source_target_pairs={{0,8},{8,16},{16,24},{24,32},{32,40},{40,48},{48,56},{56,64},{64,7... | collective-permute-start | bytes 589832 | tf_op jit(solution)/shard_map/ppermute | solution.py:16
  442.3 172.2 %collective-permute-start.5 = (f32[16,6,1,512]{3,0,2,1:T(8,128)}, f32[16,6,1,512]{3,0,2,1:T(8,128)}, u32[]{:S(2)}, u32[]{:S(2)}) collective-permute-start(f32[16,6,1,512]{3,0,2,1:T(8,128)} %get-tuple-element.56), channel_id=1, source_target_pairs={{8,0},{16,8},{24,16},{32,24},{40,32},{48,40},{56,48},{64,56},{72,6... | collective-permute-start | bytes 589832 | tf_op jit(solution)/shard_map/ppermute | solution.py:18
  535.2 82.5 %collective-permute-start.9 = (f32[16,6,1,512]{3,0,2,1:T(8,128)}, f32[16,6,1,512]{3,0,2,1:T(8,128)}, u32[]{:S(2)}, u32[]{:S(2)}) collective-permute-start(f32[16,6,1,512]{3,0,2,1:T(8,128)} %get-tuple-element.41), channel_id=1, source_target_pairs={{0,8},{8,16},{16,24},{24,32},{32,40},{40,48},{48,56},{56,64},{64,7... | collective-permute-start | bytes 589832 | tf_op jit(solution)/shard_map/ppermute | solution.py:16
  535.6 80.5 %collective-permute-start.8 = (f32[16,6,1,512]{3,0,2,1:T(8,128)}, f32[16,6,1,512]{3,0,2,1:T(8,128)}, u32[]{:S(2)}, u32[]{:S(2)}) collective-permute-start(f32[16,6,1,512]{3,0,2,1:T(8,128)} %get-tuple-element.42), channel_id=1, source_target_pairs={{8,0},{16,8},{24,16},{32,24},{40,32},{48,40},{56,48},{64,56},{72,6... | collective-permute-start | bytes 589832 | tf_op jit(solution)/shard_map/ppermute | solution.py:18
  611.2 378.9 %all-reduce.7.cloned.1.call-start = ((), (), s32[]{:S(2)}) async-start(), calls=%async_computation | async-start | bytes 393216 | tf_op jit(solution)/shard_map/psum | solution.py:163
  621.8 256.8 %copy-start.17 = (f32[16,6,1,512]{3,0,2,1:T(8,128)S(1)}, f32[16,6,1,512]{3,0,2,1:T(8,128)}, u32[]{:S(2)}) copy-start(f32[16,6,1,512]{3,0,2,1:T(8,128)} %fusion.83) | copy-start | bytes 589828
  621.8 256.8 %copy-start.19 = (f32[16,6,1,512]{3,0,2,1:T(8,128)S(1)}, f32[16,6,1,512]{3,0,2,1:T(8,128)}, u32[]{:S(2)}) copy-start(f32[16,6,1,512]{3,0,2,1:T(8,128)} %maximum_select_fusion.1) | copy-start | bytes 589828
  897.5 94.2 %copy-start.1 = (bf16[4,6,16,512]{3,2,1,0:T(8,128)(2,1)S(1)}, bf16[4,6,16,512]{3,2,1,0:T(8,128)(2,1)}, u32[]{:S(2)}) copy-start(bf16[4,6,16,512]{3,2,1,0:T(8,128)(2,1)} %param.8) | copy-start | bytes 1179652
  (26 other events, 391.1 us)
Sparse Core Ops, SparseCore 0:
  32.6 219.4 all-reduce.10
  611.3 217.6 all-reduce.8
  905.3 84.7 all-reduce.6
where the time goes:
time: 1020 us; the launch traced here: 999 us
  local copies, waits for them, and re-layouts  349 us (34%)
  waiting for transfers between devices  288 us (28%)
  blocking collectives  240 us (24%)
  other arithmetic  54.9 us (5%)
  matrix products  32.5 us (3%)
  starting transfers between devices  20.3 us (2%)
  between operations  14.1 us (1%)
    psum x2, waiting for transfers between devices, from_root(): return lax.psum(kept, axis)  203 us
    all_gather x5, blocking collectives, fill_rims(): gathered = lax.all_gather(edge_stack, 'tile', axis=2, tiled=True)  182 us
    unnamed x164, local copies, waits for them, and re-layouts  107 us
    psum x1, waiting for transfers between devices, body(): summed = lax.psum(grad_late + grad_early, 'samp')  84.9 us
    psum x1, blocking collectives, from_root(): return lax.psum(kept, axis)  58.2 us
    rev x30, local copies, waits for them, and re-layouts, window_back(): return window(line, mirror)[..., ::-1]  31.2 us
    dynamic_slice x42, local copies, waits for them, and re-layouts, window(): return lax.dynamic_slice_in_dim(line, at, local_width, axis=line.ndim - 1)  29.6 us
    reduce_sum x2, other arithmetic, edge_term(): return 0.5 * jnp.sum(summed, axis=0)  25.6 us
  transfers between devices with their start and end apart: 13, of which 2 were waited for; matrix products, arithmetic and copies ran while one was open for 28% of the time, Pallas kernels for 0%

commit v1 on v0

v1 whole, which is shorter than its diff:
```python
import jax
import jax.numpy as jnp
from jax import lax
from jax.experimental import pallas as pl
from jax.experimental.pallas import tpu as pltpu
from jax.sharding import PartitionSpec as P

F32, BF16 = jnp.float32, jnp.bfloat16
MESH = pl.DeviceIdType.MESH
TILES, SAMPS, ROWS, CELLS, LAYERS, PANELS = 32, 8, 16, 512, 16, 6
LAST = TILES - 1


def split(x):
    high = x.astype(BF16)
    return high, (x - high.astype(F32)).astype(BF16)


def iota(shape, axis):
    return lax.broadcasted_iota(jnp.int32, shape, axis)


def dot(a, b):
    return jnp.dot(a, b, preferred_element_type=F32)


def kernel(
    depth_hbm, state_hbm, pattern_hbm, index_ref, coupling_ref, weight_hbm, out_ref,
    xs, ws, ps, bs, kz, kv, kq, field, qf, acc, ocs, pk, colh, gath, scat, prow, precv,
    mirror_out, mirror_in, hub_out, gath_p, scat_p, hub_in, part, rs_in, ag, done,
    load_x, load_w, load_pb, row_send, row_recv, hub_send, gath_recv, mir_send, mir_recv,
    scat_send, scat_recv, p_send, p_recv, pm_send, pm_recv, ph_send, pgath_recv, ps_send, ps_recv,
    rs_send, rs_recv, ag_send, ag_recv,
):
    t = lax.axis_index("tile")
    s = lax.axis_index("samp")
    left, right, mirror = (t + LAST) % TILES, (t + 1) % TILES, LAST - t
    is_first, is_last = t == 0, t == LAST
    is_hub = jnp.logical_or(is_first, is_last)
    at_end = t // LAST
    at_start = mirror // LAST

    barrier = pltpu.get_barrier_semaphore()

    def greet(device):
        pl.semaphore_signal(barrier, inc=1, device_id=device, device_id_type=MESH)

    def tell_tile(u, c):
        @pl.when(u != t)
        def _():
            greet({"tile": u})
        return c

    lax.fori_loop(0, TILES, tell_tile, 0)

    def tell_samp(u, c):
        @pl.when(u != s)
        def _():
            greet({"samp": u})
        return c

    lax.fori_loop(0, SAMPS, tell_samp, 0)

    def load(p):
        return (
            pltpu.make_async_copy(state_hbm.at[:, p], xs.at[p], load_x.at[p]),
            pltpu.make_async_copy(weight_hbm.at[0, :, p], ws.at[p], load_w.at[p]),
        )

    def panel_at(step):
        return jnp.minimum(1 + 2 * step, 10 - 2 * step)

    load_p = pltpu.make_async_copy(pattern_hbm, ps, load_pb.at[0])
    load_b = pltpu.make_async_copy(depth_hbm, bs, load_pb.at[1])
    for step in range(PANELS):
        for copy in load(min(1 + 2 * step, 10 - 2 * step)):
            copy.start()
        if step == 0:
            load_p.start()
            load_b.start()

    mixing = coupling_ref[...] + jnp.where(iota((16, 16), 0) == iota((16, 16), 1), 1.0, 0.0)
    to_layer = (iota((256, 16), 0) % 16 == iota((256, 16), 1)).astype(BF16)
    from_layer = (iota((16, 256), 0) == iota((16, 256), 1) // 16).astype(BF16)
    same_row = iota((256, 256), 0) // 16 == iota((256, 256), 1) % 16

    def spread(matrix):
        tall = dot(to_layer, matrix).astype(BF16)
        return jnp.where(same_row, dot(tall, from_layer), 0.0).astype(BF16)

    for target, matrix in ((kz, mixing), (kv, mixing.T)):
        high, low = split(matrix)
        spread_high = spread(high)
        target[:, 0:256] = spread_high
        target[:, 256:512] = spread(low)
        target[:, 512:768] = spread_high
    thirty = jnp.where(
        jnp.logical_and(same_row, iota((256, 256), 0) % 16 == iota((256, 256), 1) // 16), 30.0, 0.0
    ).astype(BF16)
    kq[:, 0:256] = thirty
    kq[:, 256:512] = thirty
    chosen = (iota((4, 16), 0) == jnp.broadcast_to(index_ref[...], (4, 16))).astype(F32)
    tall = lax.dot_general(
        to_layer, chosen.astype(BF16), (((1,), (1,)), ((), ())), preferred_element_type=F32
    ).astype(BF16)
    from_pattern = (iota((4, 64), 0) == iota((4, 64), 1) // 16).astype(BF16)
    kq[:, 512:576] = jnp.where(
        iota((256, 64), 0) // 16 == iota((256, 64), 1) % 16, dot(tall, from_pattern), 0.0
    ).astype(BF16)

    acc[...] = jnp.zeros_like(acc)
    lanes = iota((8, 128), 1)
    pl.semaphore_wait(barrier, TILES - 1 + SAMPS - 1)

    def remote(src, dst, send, recv, device):
        return pltpu.make_async_remote_copy(
            src_ref=src, dst_ref=dst, send_sem=send, recv_sem=recv,
            device_id=device, device_id_type=MESH,
        )

    def row_south(p):
        to = p + jnp.where(p < 4, at_end * ((p + 1) % 4 - p), 0)
        return remote(field.at[p, 16], field.at[to, 0], row_send.at[0, p], row_recv.at[0, to], {"tile": right})

    def row_north(p):
        to = p + jnp.where(p < 4, at_start * ((p + 3) % 4 - p), 0)
        return remote(field.at[p, 1], field.at[to, 17], row_send.at[1, p], row_recv.at[1, to], {"tile": left})

    def came_from_left(p):
        return remote(field.at[p, 16], field.at[p, 0], row_send.at[0, p], row_recv.at[0, p], {"tile": right})

    def came_from_right(p):
        return remote(field.at[p, 1], field.at[p, 17], row_send.at[1, p], row_recv.at[1, p], {"tile": left})

    def south_goes(p):
        return jnp.logical_or(p < 4, jnp.logical_not(is_last))

    def north_goes(p):
        return jnp.logical_or(p < 4, jnp.logical_not(is_first))

    def gather_to(hub):
        panel = 1 if hub else 3
        return remote(pk.at[panel], gath.at[t], hub_send.at[panel // 2], gath_recv.at[t], {"tile": hub})

    MIRRORED = (((2, 0), (5, 0)), ((2, 1), (4, 1)), ((5, 0), (2, 0)), ((4, 1), (2, 1)))

    def mirrored(n):
        (a, b), (c, d) = MIRRORED[n]
        return remote(pk.at[a, b], colh.at[c, d], mir_send.at[n], mir_recv.at[n], {"tile": mirror})

    def scatter_to(u, panel):
        return remote(scat.at[u], colh.at[panel], scat_send.at[u], scat_recv.at[panel // 2], {"tile": u})

    def seg_w(u):
        return jnp.where(is_last, LAST - u, u)

    def seg_e(u):
        return jnp.where(is_last, u, LAST - u)

    def make_scatter():
        slot = jnp.where(is_last, 16, 1)

        def one(u, c):
            for side in range(2):
                seg = seg_e(u) if side else seg_w(u)
                block, place = seg // 8, seg % 8
                out = jnp.zeros((8, 128), F32)
                for g in range(5):
                    x = field[5 - side, slot, pl.ds(8 * g, 8), pl.ds(pl.multiple_of(block * 128, 128), 128)]
                    x = pltpu.roll(x, (16 * g - 16 * place + 128) % 128, 1)
                    out = jnp.where(lanes // 16 == g, x, out)
                scat[u, side] = out

            @pl.when(jnp.logical_and(u != t, is_last))
            def _():
                scatter_to(u, 1).start()

            @pl.when(jnp.logical_and(u != t, is_first))
            def _():
                scatter_to(u, 3).start()

            return c

        lax.fori_loop(0, TILES, one, 0)

        @pl.when(is_last)
        def _():
            colh[1] = scat[t]

        @pl.when(is_first)
        def _():
            colh[3] = scat[t]

    def mix(step, c):
        p = panel_at(step)
        for copy in load(p):
            copy.wait()
        xh, xl = split(xs[p].reshape(256, CELLS))
        z = dot(kz[...], jnp.concatenate([xh, xh, xl], 0))
        field[p, 1:17, 0:16, :] = z.reshape(ROWS, 16, CELLS)
        pat = ps[:, p].reshape(64, CELLS)
        q = dot(kq[...], jnp.concatenate([xh, xl, pat], 0))
        qf[p] = q.reshape(ROWS, 16, CELLS)
        wh, wl = split(ws[p].reshape(256, CELLS))
        v = dot(kv[...], jnp.concatenate([wh, wh, wl], 0))
        field[p, 1:17, 16:32, :] = v.reshape(ROWS, 16, CELLS)
        for i in range(ROWS):
            field[p, 1 + i, 32:40, :] = jnp.broadcast_to(0.5 * bs[p, i : i + 1, :], (8, CELLS))

        @pl.when(south_goes(p))
        def _():
            row_south(p).start()

        @pl.when(north_goes(p))
        def _():
            row_north(p).start()

        for side in range(2):
            if side == 0:
                rev = jnp.where(jnp.logical_or(p == 1, jnp.logical_or(p == 2, p == 5)), 1, 0)
            else:
                rev = jnp.where(jnp.logical_and(p >= 2, p <= 4), 1, 0)
            out = jnp.zeros((8, 128), F32)
            for i in range(ROWS):
                for g in range(5):
                    if side == 0:
                        x = field[p, 1 + i, 8 * g : 8 * g + 8, 0:128][:, 0:1]
                    else:
                        x = field[p, 1 + i, 8 * g : 8 * g + 8, CELLS - 128 : CELLS][:, 127:128]
                    spot = 16 * g + i + rev * (15 - 2 * i)
                    out = jnp.where(lanes == spot, jnp.broadcast_to(x, (8, 128)), out)
            pk[p, side] = out

        for at, hub in ((0, LAST), (1, 0)):
            @pl.when(jnp.logical_and(step == at, t != hub))
            def _():
                gather_to(hub).start()

            @pl.when(jnp.logical_and(step == at, t == hub))
            def _():
                gath[t] = pk[1 if hub else 3]

        @pl.when(jnp.logical_and(step == 3, is_hub))
        def _():
            make_scatter()

        return c

    load_p.wait()
    load_b.wait()
    lax.fori_loop(0, PANELS, mix, 0)

    for n in range(4):
        mirrored(n).start()
    colh[0, 0] = pk[5, 1]
    colh[0, 1] = pk[4, 0]
    colh[4, 0] = pk[0, 1]
    colh[5, 1] = pk[0, 0]

    first_lane, last_lane = lanes == 0, lanes == 127

    def blocks(x):
        return [x[:, 128 * k : 128 * k + 128] for k in range(4)]

    def to_left(b, tail):
        r = [pltpu.roll(x, 127, 1) for x in b] + [tail]
        return [jnp.where(last_lane, r[k + 1], r[k]) for k in range(4)]

    def to_right(b, head):
        r = [head] + [pltpu.roll(x, 1, 1) for x in b]
        return [jnp.where(first_lane, r[k], r[k + 1]) for k in range(4)]

    def add(a, b):
        return [x + y for x, y in zip(a, b)]

    def sub(a, b):
        return [x - y for x, y in zip(a, b)]

    def mul(a, b):
        return [x * y for x, y in zip(a, b)]

    def stencil_row(p, i):
        slot = i + 1
        west, east = colh[p, 0], colh[p, 1]
        rev_w, rev_e = jnp.where(p == 1, 1, 0), jnp.where(p == 3, 1, 0)
        lane_w = i + rev_w * (15 - 2 * i)
        lane_e = i + rev_e * (15 - 2 * i)

        def rows(g, at):
            return blocks(field[p, at, 8 * g : 8 * g + 8, :])

        def from_west(g):
            return pltpu.roll(west, (128 - 16 * g - lane_w) % 128, 1)

        def from_east(g):
            return pltpu.roll(east, (127 - 16 * g - lane_e) % 128, 1)

        h = rows(4, slot)
        beta_e = add(h, to_left(h, from_east(4)))
        beta_w = to_right(beta_e, h[0] + from_west(4))
        beta_s = add(h, rows(4, slot + 1))
        beta_n = add(h, rows(4, slot - 1))

        def lap(g):
            x = rows(g, slot)
            de = sub(to_left(x, from_east(g)), x)
            dw = to_right(de, x[0] - from_west(g))
            ds = sub(rows(g, slot + 1), x)
            dn = sub(x, rows(g, slot - 1))
            total = sub(add(mul(beta_e, de), mul(beta_s, ds)), add(mul(beta_w, dw), mul(beta_n, dn)))
            return total, de, dw, ds, dn

        sums = None
        for half in range(2):
            lz, *dz = lap(half)
            lv, *dv = lap(2 + half)
            q = add(lz, blocks(qf[p, i, 8 * half : 8 * half + 8, :]))
            terms = [add(mul(a, q), mul(b, lv)) for a, b in zip(dv, dz)]
            sums = terms if sums is None else [add(a, b) for a, b in zip(sums, terms)]
        pe, pw, ps_, pn = sums
        zero = jnp.zeros((8, 128), F32)
        own = sub(add(pe, ps_), add(pw, pn))
        move_e = to_right(pe, zero)
        move_w = to_left(pw, zero)
        own = add(own, sub(move_e, move_w))
        ocs[p, i] = jnp.where(
            first_lane, pltpu.roll(pe[3], 1, 1), jnp.where(last_lane, -pltpu.roll(pw[0], 127, 1), 0.0)
        )
        return [-x for x in pn], own, ps_

    def accumulate(p, slot, value):
        for k in range(4):
            acc[p, slot, :, 128 * k : 128 * k + 128] += value[k]

    def stencil_rows(p, start, count):
        pending = {}
        for r in range(count):
            for offset, value in enumerate(stencil_row(p, start + r)):
                key = r + offset
                pending[key] = add(pending[key], value) if key in pending else value
            accumulate(p, start + r, pending.pop(r))
        for key, value in pending.items():
            accumulate(p, start + key, value)

    def wait_columns():
        for n in range(4):
            mirrored(n).wait_recv()

        @pl.when(t != LAST)
        def _():
            scatter_to(LAST, 1).wait_recv()

        @pl.when(t != 0)
        def _():
            scatter_to(0, 3).wait_recv()

    def inner(p, c):
        @pl.when(p == 1)
        def _():
            wait_columns()

        def two(n, c):
            stencil_rows(p, 1 + 2 * n, 2)
            return c

        lax.fori_loop(0, 7, two, 0)
        return c

    lax.fori_loop(0, PANELS, inner, 0)

    @pl.when(is_hub)
    def _():
        def wait_one(u, c):
            @pl.when(u != t)
            def _():
                remote(pk.at[1], gath.at[u], hub_send.at[0], gath_recv.at[u], {"tile": u}).wait_recv()
            return c

        lax.fori_loop(0, TILES, wait_one, 0)
        slot = jnp.where(is_last, 17, 0)

        def one(block, c):
            for side in range(2):
                for g in range(5):
                    out = jnp.zeros((8, 128), F32)
                    for k in range(8):
                        seg = 8 * block + k
                        u = seg_e(seg) if side else seg_w(seg)
                        x = pltpu.roll(gath[u, side], (16 * k - 16 * g + 128) % 128, 1)
                        out = jnp.where(lanes // 16 == k, x, out)
                    field[5 - side, slot, pl.ds(8 * g, 8), pl.ds(pl.multiple_of(block * 128, 128), 128)] = out
            return c

        lax.fori_loop(0, 4, one, 0)

    def outer(p, c):
        @pl.when(jnp.logical_or(p < 4, jnp.logical_not(is_first)))
        def _():
            came_from_left(p).wait_recv()

        @pl.when(jnp.logical_or(p < 4, jnp.logical_not(is_last)))
        def _():
            came_from_right(p).wait_recv()

        stencil_rows(p, 0, 1)
        stencil_rows(p, ROWS - 1, 1)
        return c

    lax.fori_loop(0, PANELS, outer, 0)

    def fold(matrix, x):
        high, low = split(x)
        return dot(matrix, high) + dot(matrix, low)

    fold_rows = (iota((ROWS, 8 * ROWS), 0) == iota((ROWS, 8 * ROWS), 1) // 8).astype(BF16)
    fold_panels = (iota((8, 8 * PANELS), 0) == iota((8, 8 * PANELS), 1) // 8).astype(BF16)
    prow[0] = fold(fold_panels, acc[:, 0].reshape(8 * PANELS, CELLS))
    prow[1] = fold(fold_panels, acc[:, 17].reshape(8 * PANELS, CELLS))
    p_south = remote(prow.at[1], precv.at[0], p_send.at[0], p_recv.at[0], {"tile": right})
    p_north = remote(prow.at[0], precv.at[1], p_send.at[1], p_recv.at[1], {"tile": left})
    p_south.start()
    p_north.start()

    lane16, row16 = iota((16, 128), 1), iota((16, 128), 0)
    leaving = [fold(fold_rows, ocs[p].reshape(8 * ROWS, 128)) for p in range(PANELS)]

    def leaving_column(p, side):
        return leaving[p][:, 0:1] if side else leaving[p][:, 127:128]

    def leaving_row(p, side, reverse):
        spot = 15 - row16 if reverse else row16
        column = jnp.broadcast_to(leaving_column(p, side), (16, 128))
        return jnp.sum(jnp.where(lane16 == spot, column, 0.0), axis=0, keepdims=True)

    mirror_out[...] = jnp.zeros_like(mirror_out)
    for n in range(4):
        (a, b), _ = MIRRORED[n]
        mirror_out[n : n + 1, :] = leaving_row(a, b, True)
    p_mirror = remote(mirror_out, mirror_in, pm_send.at[0], pm_recv.at[0], {"tile": mirror})
    p_mirror.start()

    def gather_p(hub):
        n = 0 if hub else 1
        return remote(hub_out.at[n], gath_p.at[t], ph_send.at[n], pgath_recv.at[t], {"tile": hub})

    up, down = t % 8, (LAST - t) % 8
    for n, hub in enumerate((LAST, 0)):
        panel = 1 if hub else 3
        hub_out[n] = jnp.zeros((8, 128), F32)
        hub_out[n, 0:1, :] = pltpu.roll(leaving_row(panel, 0, bool(hub)), 16 * (down if hub else up), 1)
        hub_out[n, 1:2, :] = pltpu.roll(leaving_row(panel, 1, not hub), 16 * (up if hub else down), 1)

        @pl.when(t != hub)
        def _():
            gather_p(hub).start()

        @pl.when(t == hub)
        def _():
            gath_p[t] = hub_out[n]

    def scatter_p(u, hub):
        n = 0 if hub else 1
        return remote(scat_p.at[u // 8], hub_in.at[n], ps_send.at[u], ps_recv.at[n], {"tile": u})

    @pl.when(is_hub)
    def _():
        rows = prow[jnp.where(is_last, 1, 0)]
        for block in range(4):
            ahead = rows[:, 128 * block : 128 * block + 128]
            behind = rows[:, 128 * (3 - block) : 128 * (3 - block) + 128]
            w = jnp.where(is_last, behind, ahead)
            e = jnp.where(is_last, ahead, behind)
            scat_p[block] = jnp.zeros((8, 128), F32)
            scat_p[block, 0:1, :] = w[5:6]
            scat_p[block, 1:2, :] = e[4:5]

        def one(u, c):
            @pl.when(jnp.logical_and(u != t, is_last))
            def _():
                scatter_p(u, LAST).start()

            @pl.when(jnp.logical_and(u != t, is_first))
            def _():
                scatter_p(u, 0).start()

            return c

        lax.fori_loop(0, TILES, one, 0)

        @pl.when(is_last)
        def _():
            hub_in[0] = scat_p[t // 8]

        @pl.when(is_first)
        def _():
            hub_in[1] = scat_p[t // 8]

    for p in range(PANELS):
        part[p] = fold(fold_rows, acc[p, 1:17].reshape(8 * ROWS, CELLS))

    def add_column(p, side, column):
        if side:
            at, lane = CELLS - 128, 127
        else:
            at, lane = 0, 0
        spread_out = jnp.broadcast_to(column, (16, 128))
        part[p, :, at : at + 128] += jnp.where(lane16 == lane, spread_out, 0.0)

    add_column(5, 1, leaving_column(0, 0))
    add_column(4, 0, leaving_column(0, 1))
    add_column(0, 1, leaving_column(4, 0))
    add_column(0, 0, leaving_column(5, 1))

    def row_to_column(row, base, reverse):
        spot = base + (15 - row16 if reverse else row16)
        spread_out = jnp.broadcast_to(row, (16, 128))
        return jnp.sum(jnp.where(lane16 == spot, spread_out, 0.0), axis=1, keepdims=True)

    p_south.wait_recv()
    p_north.wait_recv()
    panel_row = iota((8, CELLS), 0)
    from_north = precv[0]
    from_south = precv[1]
    pad = jnp.zeros((4, CELLS), F32)
    from_north = jnp.where(is_first, jnp.concatenate([from_north[3:4], from_north[0:3], pad], 0), from_north)
    from_south = jnp.where(is_last, jnp.concatenate([from_south[1:4], from_south[0:1], pad], 0), from_south)
    for p in range(PANELS):
        part[p, 0:1, :] += from_north[p : p + 1]
        part[p, ROWS - 1 : ROWS, :] += from_south[p : p + 1]

    p_mirror.wait_recv()
    for n in range(4):
        _, (a, b) = MIRRORED[n]
        add_column(a, b, row_to_column(mirror_in[n : n + 1, :], 0, False))

    @pl.when(t != LAST)
    def _():
        scatter_p(LAST, LAST).wait_recv()

    @pl.when(t != 0)
    def _():
        scatter_p(0, 0).wait_recv()

    add_column(1, 0, row_to_column(hub_in[0, 0:1, :], 16 * down, True))
    add_column(1, 1, row_to_column(hub_in[0, 1:2, :], 16 * up, False))
    add_column(3, 0, row_to_column(hub_in[1, 0:1, :], 16 * up, False))
    add_column(3, 1, row_to_column(hub_in[1, 1:2, :], 16 * down, True))

    @pl.when(is_hub)
    def _():
        def wait_one(u, c):
            @pl.when(u != t)
            def _():
                remote(hub_out.at[0], gath_p.at[u], ph_send.at[0], pgath_recv.at[u], {"tile": u}).wait_recv()
            return c

        lax.fori_loop(0, TILES, wait_one, 0)

        def hub_row(block, side):
            total = jnp.zeros((8, 128), F32)
            for k in range(8):
                seg = 8 * block + k
                total = total + gath_p[seg_e(seg) if side else seg_w(seg)]
            return total[side : side + 1, :]

        for block in range(4):
            for side in range(2):
                row = hub_row(block, side)
                at = 128 * block

                @pl.when(is_last)
                def _():
                    part[5 - side, ROWS - 1 : ROWS, at : at + 128] += row

                @pl.when(is_first)
                def _():
                    part[5 - side, 0:1, at : at + 128] += row

    for n in range(SAMPS):
        h, k = n // 4, n % 4
        rs_in[n] = part[:, 8 * h : 8 * h + 8, 128 * k : 128 * k + 128]

    def each_peer(fn):
        def one(d, c):
            fn((s + d) % SAMPS)
            return c

        lax.fori_loop(1, SAMPS, one, 0)

    def reduce_to(peer):
        return remote(rs_in.at[peer], ag.at[s], rs_send.at[peer], rs_recv.at[s], {"samp": peer})

    def reduce_from(peer):
        return remote(rs_in.at[peer], ag.at[peer], rs_send.at[peer], rs_recv.at[peer], {"samp": peer})

    each_peer(lambda peer: reduce_to(peer).start())
    ag[s] = rs_in[s]
    each_peer(lambda peer: reduce_from(peer).wait_recv())
    each_peer(lambda peer: reduce_to(peer).wait_send())
    total = ag[0]
    for n in range(1, SAMPS):
        total = total + ag[n]
    done[s] = total * (0.005 / SAMPS)

    def share_with(peer):
        return remote(done.at[s], done.at[s], ag_send.at[peer], ag_recv.at[s], {"samp": peer})

    def share_from(peer):
        return remote(done.at[peer], done.at[peer], ag_send.at[peer], ag_recv.at[peer], {"samp": peer})

    each_peer(lambda peer: share_with(peer).start())
    each_peer(lambda peer: share_from(peer).wait_recv())
    for n in range(SAMPS):
        h, k = n // 4, n % 4
        out_ref[:, 8 * h : 8 * h + 8, 128 * k : 128 * k + 128] = done[n]

    each_peer(lambda peer: share_with(peer).wait_send())
    for p in range(PANELS):
        @pl.when(south_goes(p))
        def _():
            row_south(p).wait_send()

        @pl.when(north_goes(p))
        def _():
            row_north(p).wait_send()

    for n in range(4):
        mirrored(n).wait_send()
    p_south.wait_send()
    p_north.wait_send()
    p_mirror.wait_send()
    for hub in (LAST, 0):
        @pl.when(t != hub)
        def _():
            gather_to(hub).wait_send()
            gather_p(hub).wait_send()

    @pl.when(is_hub)
    def _():
        def one(u, c):
            @pl.when(u != t)
            def _():
                scatter_to(u, 1).wait_send()
                scatter_p(u, LAST).wait_send()
            return c

        lax.fori_loop(0, TILES, one, 0)


def body(bathymetry, initial_state, patterns, pattern_index, coupling, final_weights):
    vmem = pl.BlockSpec(memory_space=pltpu.VMEM)
    hbm = pl.BlockSpec(memory_space=pl.ANY)
    tile = (8, 128)
    dma = pltpu.SemaphoreType.DMA
    return pl.pallas_call(
        kernel,
        out_shape=jax.ShapeDtypeStruct((PANELS, ROWS, CELLS), F32),
        in_specs=[hbm, hbm, hbm, vmem, vmem, hbm],
        out_specs=vmem,
        scratch_shapes=[
            pltpu.VMEM((PANELS, LAYERS, ROWS, CELLS), F32),
            pltpu.VMEM((PANELS, LAYERS, ROWS, CELLS), F32),
            pltpu.VMEM((4, PANELS, ROWS, CELLS), BF16),
            pltpu.VMEM((PANELS, ROWS, CELLS), F32),
            pltpu.VMEM((256, 768), BF16),
            pltpu.VMEM((256, 768), BF16),
            pltpu.VMEM((256, 576), BF16),
            pltpu.VMEM((PANELS, ROWS + 2, 40, CELLS), F32),
            pltpu.VMEM((PANELS, ROWS, LAYERS, CELLS), F32),
            pltpu.VMEM((PANELS, ROWS + 2, 8, CELLS), F32),
            pltpu.VMEM((PANELS, ROWS) + tile, F32),
            pltpu.VMEM((PANELS, 2) + tile, F32),
            pltpu.VMEM((PANELS, 2) + tile, F32),
            pltpu.VMEM((TILES, 2) + tile, F32),
            pltpu.VMEM((TILES, 2) + tile, F32),
            pltpu.VMEM((2, 8, CELLS), F32),
            pltpu.VMEM((2, 8, CELLS), F32),
            pltpu.VMEM(tile, F32),
            pltpu.VMEM(tile, F32),
            pltpu.VMEM((2,) + tile, F32),
            pltpu.VMEM((TILES,) + tile, F32),
            pltpu.VMEM((4,) + tile, F32),
            pltpu.VMEM((2,) + tile, F32),
            pltpu.VMEM((PANELS, ROWS, CELLS), F32),
            pltpu.VMEM((SAMPS, PANELS) + tile, F32),
            pltpu.VMEM((SAMPS, PANELS) + tile, F32),
            pltpu.VMEM((SAMPS, PANELS) + tile, F32),
            dma((PANELS,)), dma((PANELS,)), dma((2,)),
            dma((2, PANELS)), dma((2, PANELS)),
            dma((2,)), dma((TILES,)), dma((4,)), dma((4,)),
            dma((TILES,)), dma((2,)),
            dma((2,)), dma((2,)), dma((1,)), dma((1,)),
            dma((2,)), dma((TILES,)), dma((TILES,)), dma((2,)),
            dma((SAMPS,)), dma((SAMPS,)), dma((SAMPS,)), dma((SAMPS,)),
        ],
        compiler_params=pltpu.CompilerParams(
            collective_id=0, has_side_effects=True, vmem_limit_bytes=48 * 1024 * 1024
        ),
        cost_estimate=pl.CostEstimate(flops=200_000_000, bytes_accessed=7_000_000, transcendentals=0),
    )(bathymetry, initial_state, patterns, pattern_index, coupling, final_weights)


def solution(mesh):
    in_specs = (
        P(None, "tile", None),
        P(None, None, "tile", None),
        P(None, None, "tile", None),
        P("samp", None),
        P(),
        P("samp", None, None, "tile", None),
    )
    out_specs = P(None, "tile", None)
    return jax.shard_map(body, mesh=mesh, in_specs=in_specs, out_specs=out_specs, check_vma=False)
```

time: 1020 us -> 58.7 us (0.06); the launches traced: 999 us -> 58.5 us
  local copies, waits for them, and re-layouts: 349 us -> 5.84 us
  waiting for transfers between devices: 288 us -> 0 us
  blocking collectives: 240 us -> 0 us
  other arithmetic: 54.9 us -> 0 us
  Pallas kernels: 0 us -> 52.6 us
  matrix products: 32.5 us -> 0 us
  starting transfers between devices: 20.3 us -> 0 us
  between operations: 14.1 us -> 0.01 us
    psum x3 -> x0, waiting for transfers between devices: 288 us -> none  [the longest x2 203 us: from_root(): return lax.psum(kept, axis)]
    all_gather x5 -> x0, blocking collectives: 182 us -> none  [fill_rims(): gathered = lax.all_gather(edge_stack, 'tile', axis=2, tiled=True)]
    unnamed x164 -> x11, local copies, waits for them, and re-layouts: 107 us -> 5.84 us
    slice x61 -> x0, local copies, waits for them, and re-layouts: 95.9 us -> none  [the longest x2 9.43 us: fill_rims(): gathered[:, 3]]
    psum x1 -> x0, blocking collectives: 58.2 us -> none  [from_root(): return lax.psum(kept, axis)]
    pallas_call x0 -> x1, Pallas kernels: none -> 52.6 us  [body(): pl.pallas_call(kernel, out_shape=jax.ShapeDtypeStruct((PANELS, ROWS, CELL...]
    rev x40 -> x0, local copies, waits for them, and re-layouts: 47.2 us -> none  [the longest x30 31.2 us: window_back(): return window(line, mirror)[..., ::-1]]
    dot_general x4 -> x0, matrix products: 32.5 us -> none  [the longest x1 14 us: body(): jnp.einsum('km,kpij->mpij', mixing, lap_weight, precision=lax.Precision.H...]
  transfers between devices with their start and end apart: 13 -> 0, of which waited for: 2 -> 0; matrix products, arithmetic and copies ran while one was open for 28% -> 0% of each run, Pallas kernels for 0% -> 0%
where the time goes in v1:
time: 58.7 us; the launch traced here: 58.5 us
  Pallas kernels  52.6 us (90%)
  local copies, waits for them, and re-layouts  5.84 us (10%)
    pallas_call x1, Pallas kernels, body(): pl.pallas_call(kernel, out_shape=jax.ShapeDtypeStruct((PANELS, ROWS, CELL...  52.6 us
    unnamed x11, local copies, waits for them, and re-layouts  5.84 us

profile of v1, /device:TPU:4, one launch (start us, length us, event | category | flops | bytes accessed | tf_op | source)
XLA Modules:
  0.0 58.5 jit_solution(6092636819970445184)
XLA Ops:
  0.0 0.0 copy-start
  0.0 1.9 %copy-done = f32[16,6,16,512]{3,2,1,0:T(8,128)S(1)} copy-done((f32[16,6,16,512]{3,2,1,0:T(8,128)S(1)}, f32[16,6,16,512]{3,2,1,0:T(8,128)}, u32[]{:S(2)}) %copy-start) | copy-done | bytes 3145752
  1.9 0.0 copy-start.1
  1.9 1.0 %copy-done.1 = bf16[4,6,16,512]{3,2,1,0:T(8,128)(2,1)S(1)} copy-done((bf16[4,6,16,512]{3,2,1,0:T(8,128)(2,1)S(1)}, bf16[4,6,16,512]{3,2,1,0:T(8,128)(2,1)}, u32[]{:S(2)}) %copy-start.1) | copy-done | bytes 393240
  2.9 0.0 copy-start.2
  2.9 0.9 %copy-done.2 = f32[6,16,512]{2,1,0:T(8,128)S(1)} copy-done((f32[6,16,512]{2,1,0:T(8,128)S(1)}, f32[6,16,512]{2,1,0:T(8,128)}, u32[]{:S(2)}) %copy-start.2) | copy-done | bytes 196632
  3.8 0.0 copy-start.3
  3.8 0.7 %copy-done.3 = f32[16,16]{1,0:T(8,128)S(1)} copy-done((f32[16,16]{1,0:T(8,128)S(1)}, f32[16,16]{1,0:T(8,128)}, u32[]{:S(2)}) %copy-start.3) | copy-done | bytes 1048
  4.5 0.0 copy-start.4
  4.5 0.7 %copy-done.4 = s32[1,16]{1,0:T(1,128)S(1)} copy-done((s32[1,16]{1,0:T(1,128)S(1)}, s32[1,16]{1,0:T(1,128)}, u32[]{:S(2)}) %copy-start.4) | copy-done | bytes 88
  5.2 52.6 %shard_map.64 = f32[6,16,512]{2,1,0:T(8,128)S(1)} custom-call(f32[6,16,512]{2,1,0:T(8,128)S(1)} %copy-done.2, f32[16,6,16,512]{3,2,1,0:T(8,128)S(1)} %copy-done, bf16[4,6,16,512]{3,2,1,0:T(8,128)(2,1)S(1)} %copy-done.1, s32[1,16]{1,0:T(1,128)S(1)} %copy-done.4, f32[16,16]{1,0:T(8,128)S(1)} %copy-done.3, f32[1,16,6,16,512]{4,3,2,1,0:T(8,128)} %weight_hbm.1), custom_call_target="tpu_custom_call" | custom-call | flops 200000000 | bytes 7000000 | tf_op jit(solution)/shard_map/pallas_call | solution.py:655
  57.8 0.7 %copy.8 = f32[6,16,512]{2,1,0:T(8,128)} copy(f32[6,16,512]{2,1,0:T(8,128)S(1)} %shard_map.64) | data formatting | bytes 393216
Async XLA Ops:
  0.0 1.9 %copy-start = (f32[16,6,16,512]{3,2,1,0:T(8,128)S(1)}, f32[16,6,16,512]{3,2,1,0:T(8,128)}, u32[]{:S(2)}) copy-start(f32[16,6,16,512]{3,2,1,0:T(8,128)} %state_hbm.1) | copy-start | bytes 9437188
  1.9 1.0 %copy-start.1 = (bf16[4,6,16,512]{3,2,1,0:T(8,128)(2,1)S(1)}, bf16[4,6,16,512]{3,2,1,0:T(8,128)(2,1)}, u32[]{:S(2)}) copy-start(bf16[4,6,16,512]{3,2,1,0:T(8,128)(2,1)} %pattern_hbm.1) | copy-start | bytes 1179652
  2.9 0.9 %copy-start.2 = (f32[6,16,512]{2,1,0:T(8,128)S(1)}, f32[6,16,512]{2,1,0:T(8,128)}, u32[]{:S(2)}) copy-start(f32[6,16,512]{2,1,0:T(8,128)} %depth_hbm.1) | copy-start | bytes 589828
  3.8 0.7 %copy-start.3 = (f32[16,16]{1,0:T(8,128)S(1)}, f32[16,16]{1,0:T(8,128)}, u32[]{:S(2)}) copy-start(f32[16,16]{1,0:T(8,128)} %coupling_ref.1) | copy-start | bytes 3076
  4.5 0.7 %copy-start.4 = (s32[1,16]{1,0:T(1,128)S(1)}, s32[1,16]{1,0:T(1,128)}, u32[]{:S(2)}) copy-start(s32[1,16]{1,0:T(1,128)} %index_ref.1) | copy-start | bytes 196

commit v2 on v1

--- a/solution.py
+++ b/solution.py
@@ -26,7 +26,7 @@
 
 def kernel(
     depth_hbm, state_hbm, pattern_hbm, index_ref, coupling_ref, weight_hbm, out_ref,
-    xs, ws, ps, bs, kz, kv, kq, field, qf, acc, ocs, pk, colh, gath, scat, prow, precv,
+    xs, ws, ps, bs, kz, kv, kq, field, qf, acc, acc_s, acc_n, ocs, leaving, pk, colh, gath, scat, prow, precv,
     mirror_out, mirror_in, hub_out, gath_p, scat_p, hub_in, part, rs_in, ag, done,
     load_x, load_w, load_pb, row_send, row_recv, hub_send, gath_recv, mir_send, mir_recv,
     scat_send, scat_recv, p_send, p_recv, pm_send, pm_recv, ph_send, pgath_recv, ps_send, ps_recv,
@@ -40,44 +40,41 @@
     at_end = t // LAST
     at_start = mirror // LAST
 
-    barrier = pltpu.get_barrier_semaphore()
-
-    def greet(device):
-        pl.semaphore_signal(barrier, inc=1, device_id=device, device_id_type=MESH)
-
-    def tell_tile(u, c):
-        @pl.when(u != t)
-        def _():
-            greet({"tile": u})
-        return c
-
-    lax.fori_loop(0, TILES, tell_tile, 0)
-
-    def tell_samp(u, c):
-        @pl.when(u != s)
-        def _():
-            greet({"samp": u})
-        return c
-
-    lax.fori_loop(0, SAMPS, tell_samp, 0)
-
     def load(p):
         return (
             pltpu.make_async_copy(state_hbm.at[:, p], xs.at[p], load_x.at[p]),
             pltpu.make_async_copy(weight_hbm.at[0, :, p], ws.at[p], load_w.at[p]),
         )
 
-    def panel_at(step):
-        return jnp.minimum(1 + 2 * step, 10 - 2 * step)
-
     load_p = pltpu.make_async_copy(pattern_hbm, ps, load_pb.at[0])
     load_b = pltpu.make_async_copy(depth_hbm, bs, load_pb.at[1])
     for step in range(PANELS):
-        for copy in load(min(1 + 2 * step, 10 - 2 * step)):
+        for copy in load(PANELS - 1 - step):
             copy.start()
         if step == 0:
             load_p.start()
             load_b.start()
+
+    barrier = pltpu.get_barrier_semaphore()
+
+    def greet(device):
+        pl.semaphore_signal(barrier, inc=1, device_id=device, device_id_type=MESH)
+
+    def tell_tile(u, c):
+        @pl.when(u != t)
+        def _():
+            greet({"tile": u})
+        return c
+
+    lax.fori_loop(0, TILES, tell_tile, 0)
+
+    def tell_samp(u, c):
+        @pl.when(u != s)
+        def _():
+            greet({"samp": u})
+        return c
+
+    lax.fori_loop(0, SAMPS, tell_samp, 0)
 
     mixing = coupling_ref[...] + jnp.where(iota((16, 16), 0) == iota((16, 16), 1), 1.0, 0.0)
     to_layer = (iota((256, 16), 0) % 16 == iota((256, 16), 1)).astype(BF16)
@@ -108,9 +105,9 @@
         iota((256, 64), 0) // 16 == iota((256, 64), 1) % 16, dot(tall, from_pattern), 0.0
     ).astype(BF16)
 
-    acc[...] = jnp.zeros_like(acc)
+    acc_s[:, 1] = jnp.zeros((PANELS, 8, CELLS), F32)
+    acc_n[:, 16] = jnp.zeros((PANELS, 8, CELLS), F32)
     lanes = iota((8, 128), 1)
-    pl.semaphore_wait(barrier, TILES - 1 + SAMPS - 1)
 
     def remote(src, dst, send, recv, device):
         return pltpu.make_async_remote_copy(
@@ -192,7 +189,7 @@
             colh[3] = scat[t]
 
     def mix(step, c):
-        p = panel_at(step)
+        p = PANELS - 1 - step
         for copy in load(p):
             copy.wait()
         xh, xl = split(xs[p].reshape(256, CELLS))
@@ -206,6 +203,10 @@
         field[p, 1:17, 16:32, :] = v.reshape(ROWS, 16, CELLS)
         for i in range(ROWS):
             field[p, 1 + i, 32:40, :] = jnp.broadcast_to(0.5 * bs[p, i : i + 1, :], (8, CELLS))
+
+        @pl.when(step == 0)
+        def _():
+            pl.semaphore_wait(barrier, TILES - 1 + SAMPS - 1)
 
         @pl.when(south_goes(p))
         def _():
@@ -231,7 +232,7 @@
                     out = jnp.where(lanes == spot, jnp.broadcast_to(x, (8, 128)), out)
             pk[p, side] = out
 
-        for at, hub in ((0, LAST), (1, 0)):
+        for at, hub in ((4, LAST), (2, 0)):
             @pl.when(jnp.logical_and(step == at, t != hub))
             def _():
                 gather_to(hub).start()
@@ -240,9 +241,14 @@
             def _():
                 gath[t] = pk[1 if hub else 3]
 
-        @pl.when(jnp.logical_and(step == 3, is_hub))
+        @pl.when(jnp.logical_and(step == 1, is_hub))
         def _():
             make_scatter()
+
+        @pl.when(step == 5)
+        def _():
+            for n in range(4):
+                mirrored(n).start()
 
         return c
 
@@ -250,8 +256,6 @@
     load_b.wait()
     lax.fori_loop(0, PANELS, mix, 0)
 
-    for n in range(4):
-        mirrored(n).start()
     colh[0, 0] = pk[5, 1]
     colh[0, 1] = pk[4, 0]
     colh[4, 0] = pk[0, 1]
@@ -259,88 +263,83 @@
 
     first_lane, last_lane = lanes == 0, lanes == 127
 
-    def blocks(x):
-        return [x[:, 128 * k : 128 * k + 128] for k in range(4)]
-
-    def to_left(b, tail):
-        r = [pltpu.roll(x, 127, 1) for x in b] + [tail]
-        return [jnp.where(last_lane, r[k + 1], r[k]) for k in range(4)]
-
-    def to_right(b, head):
-        r = [head] + [pltpu.roll(x, 1, 1) for x in b]
-        return [jnp.where(first_lane, r[k], r[k + 1]) for k in range(4)]
-
-    def add(a, b):
-        return [x + y for x, y in zip(a, b)]
-
-    def sub(a, b):
-        return [x - y for x, y in zip(a, b)]
-
-    def mul(a, b):
-        return [x * y for x, y in zip(a, b)]
+    def block(g, p, slot, k):
+        return field[p, slot, 8 * g : 8 * g + 8, 128 * k : 128 * k + 128]
 
     def stencil_row(p, i):
         slot = i + 1
         west, east = colh[p, 0], colh[p, 1]
-        rev_w, rev_e = jnp.where(p == 1, 1, 0), jnp.where(p == 3, 1, 0)
-        lane_w = i + rev_w * (15 - 2 * i)
-        lane_e = i + rev_e * (15 - 2 * i)
-
-        def rows(g, at):
-            return blocks(field[p, at, 8 * g : 8 * g + 8, :])
-
-        def from_west(g):
-            return pltpu.roll(west, (128 - 16 * g - lane_w) % 128, 1)
-
-        def from_east(g):
-            return pltpu.roll(east, (127 - 16 * g - lane_e) % 128, 1)
-
-        h = rows(4, slot)
-        beta_e = add(h, to_left(h, from_east(4)))
-        beta_w = to_right(beta_e, h[0] + from_west(4))
-        beta_s = add(h, rows(4, slot + 1))
-        beta_n = add(h, rows(4, slot - 1))
-
-        def lap(g):
-            x = rows(g, slot)
-            de = sub(to_left(x, from_east(g)), x)
-            dw = to_right(de, x[0] - from_west(g))
-            ds = sub(rows(g, slot + 1), x)
-            dn = sub(x, rows(g, slot - 1))
-            total = sub(add(mul(beta_e, de), mul(beta_s, ds)), add(mul(beta_w, dw), mul(beta_n, dn)))
-            return total, de, dw, ds, dn
-
-        sums = None
-        for half in range(2):
-            lz, *dz = lap(half)
-            lv, *dv = lap(2 + half)
-            q = add(lz, blocks(qf[p, i, 8 * half : 8 * half + 8, :]))
-            terms = [add(mul(a, q), mul(b, lv)) for a, b in zip(dv, dz)]
-            sums = terms if sums is None else [add(a, b) for a, b in zip(sums, terms)]
-        pe, pw, ps_, pn = sums
-        zero = jnp.zeros((8, 128), F32)
-        own = sub(add(pe, ps_), add(pw, pn))
-        move_e = to_right(pe, zero)
-        move_w = to_left(pw, zero)
-        own = add(own, sub(move_e, move_w))
-        ocs[p, i] = jnp.where(
-            first_lane, pltpu.roll(pe[3], 1, 1), jnp.where(last_lane, -pltpu.roll(pw[0], 127, 1), 0.0)
-        )
-        return [-x for x in pn], own, ps_
-
-    def accumulate(p, slot, value):
+        at = {}
+
+        def here(g, k):
+            if (g, k) not in at:
+                x = block(g, p, slot, k)
+                at[g, k] = x, pltpu.roll(x, 127, 1)
+            return at[g, k]
+
+        def east_of(g, k):
+            x, turned = here(g, k)
+            if k < 3:
+                after = here(g, k + 1)[1]
+            else:
+                after = pltpu.roll(east, (127 - 16 * g - i) % 128, 1)
+            return x, jnp.where(last_lane, after, turned)
+
+        before = {}
+
+        def west_of(g, k, value, x):
+            turned = pltpu.roll(value, 1, 1)
+            if k == 0:
+                edge = pltpu.roll(west, (128 - 16 * g - i) % 128, 1)
+                edge = x + edge if g == 4 else x - edge
+            else:
+                edge = before[g]
+            before[g] = turned
+            return jnp.where(first_lane, edge, turned)
+
+        held = {}
         for k in range(4):
-            acc[p, slot, :, 128 * k : 128 * k + 128] += value[k]
+            x, e = east_of(4, k)
+            beta_e = x + e
+            beta_w = west_of(4, k, beta_e, x)
+            beta_s = x + block(4, p, slot + 1, k)
+            beta_n = x + block(4, p, slot - 1, k)
+            sums = None
+            for half in range(2):
+                both = []
+                for g in (half, 2 + half):
+                    x, e = east_of(g, k)
+                    de = e - x
+                    dw = west_of(g, k, de, x)
+                    ds = block(g, p, slot + 1, k) - x
+                    dn = x - block(g, p, slot - 1, k)
+                    lap = (beta_e * de - beta_w * dw) + (beta_s * ds - beta_n * dn)
+                    both.append((lap, de, dw, ds, dn))
+                (lz, *dz), (lv, *dv) = both
+                q = lz + qf[p, i, 8 * half : 8 * half + 8, 128 * k : 128 * k + 128]
+                terms = [x * q + y * lv for x, y in zip(dv, dz)]
+                sums = terms if sums is None else [x + y for x, y in zip(sums, terms)]
+            pe, pw, p_s, p_n = sums
+            cols = slice(128 * k, 128 * k + 128)
+            acc_s[p, slot + 1, :, cols] = p_s
+            acc_n[p, slot - 1, :, cols] = p_n
+            own = (pe + p_s) - (pw + p_n)
+            pe_turned = pltpu.roll(pe, 1, 1)
+            own = own + jnp.where(first_lane, held["e"] if k else 0.0, pe_turned)
+            pw_turned = pltpu.roll(pw, 127, 1)
+            if k == 0:
+                first = pw_turned
+            else:
+                acc[p, slot, :, 128 * k - 128 : 128 * k] = held["own"] - jnp.where(
+                    last_lane, pw_turned, held["w"]
+                )
+            held = {"e": pe_turned, "w": pw_turned, "own": own}
+        acc[p, slot, :, 384:512] = held["own"] - jnp.where(last_lane, 0.0, held["w"])
+        ocs[p, i] = jnp.where(first_lane, held["e"], jnp.where(last_lane, -first, 0.0))
 
     def stencil_rows(p, start, count):
-        pending = {}
         for r in range(count):
-            for offset, value in enumerate(stencil_row(p, start + r)):
-                key = r + offset
-                pending[key] = add(pending[key], value) if key in pending else value
-            accumulate(p, start + r, pending.pop(r))
-        for key, value in pending.items():
-            accumulate(p, start + key, value)
+            stencil_row(p, start + r)
 
     def wait_columns():
         for n in range(4):
@@ -354,6 +353,16 @@
         def _():
             scatter_to(0, 3).wait_recv()
 
+        turn(1, 0)
+        turn(3, 1)
+
+    def turn(p, side):
+        x = colh[p, side]
+        out = x
+        for e in range(16):
+            out = jnp.where(lanes % 16 == 15 - e, pltpu.roll(x, (15 - 2 * e) % 128, 1), out)
+        colh[p, side] = out
+
     def inner(p, c):
         @pl.when(p == 1)
         def _():
@@ -366,7 +375,7 @@
         lax.fori_loop(0, 7, two, 0)
         return c
 
-    lax.fori_loop(0, PANELS, inner, 0)
+    lax.fori_loop(0, 4, inner, 0)
 
     @pl.when(is_hub)
     def _():
@@ -414,15 +423,20 @@
 
     fold_rows = (iota((ROWS, 8 * ROWS), 0) == iota((ROWS, 8 * ROWS), 1) // 8).astype(BF16)
     fold_panels = (iota((8, 8 * PANELS), 0) == iota((8, 8 * PANELS), 1) // 8).astype(BF16)
-    prow[0] = fold(fold_panels, acc[:, 0].reshape(8 * PANELS, CELLS))
-    prow[1] = fold(fold_panels, acc[:, 17].reshape(8 * PANELS, CELLS))
+    lane16, row16 = iota((16, 128), 1), iota((16, 128), 0)
+
+    prow[0] = -fold(fold_panels, acc_n[:, 0].reshape(8 * PANELS, CELLS))
+    prow[1] = fold(fold_panels, acc_s[:, 17].reshape(8 * PANELS, CELLS))
     p_south = remote(prow.at[1], precv.at[0], p_send.at[0], p_recv.at[0], {"tile": right})
     p_north = remote(prow.at[0], precv.at[1], p_send.at[1], p_recv.at[1], {"tile": left})
     p_south.start()
     p_north.start()
 
-    lane16, row16 = iota((16, 128), 1), iota((16, 128), 0)
-    leaving = [fold(fold_rows, ocs[p].reshape(8 * ROWS, 128)) for p in range(PANELS)]
+    def fold_leaving(p, c):
+        leaving[p] = fold(fold_rows, ocs[p].reshape(8 * ROWS, 128))
+        return c
+
+    lax.fori_loop(1, 4, fold_leaving, 0)
 
     def leaving_column(p, side):
         return leaving[p][:, 0:1] if side else leaving[p][:, 127:128]
@@ -432,12 +446,17 @@
         column = jnp.broadcast_to(leaving_column(p, side), (16, 128))
         return jnp.sum(jnp.where(lane16 == spot, column, 0.0), axis=0, keepdims=True)
 
-    mirror_out[...] = jnp.zeros_like(mirror_out)
-    for n in range(4):
-        (a, b), _ = MIRRORED[n]
-        mirror_out[n : n + 1, :] = leaving_row(a, b, True)
-    p_mirror = remote(mirror_out, mirror_in, pm_send.at[0], pm_recv.at[0], {"tile": mirror})
-    p_mirror.start()
+    def p_mirror(m):
+        return remote(mirror_out.at[m], mirror_in.at[m], pm_send.at[m], pm_recv.at[m], {"tile": mirror})
+
+    def send_mirror(m):
+        mirror_out[m] = jnp.zeros((8, 128), F32)
+        for n in range(2):
+            (a, b), _ = MIRRORED[2 * m + n]
+            mirror_out[m, n : n + 1, :] = leaving_row(a, b, True)
+        p_mirror(m).start()
+
+    send_mirror(0)
 
     def gather_p(hub):
         n = 0 if hub else 1
@@ -465,14 +484,14 @@
     @pl.when(is_hub)
     def _():
         rows = prow[jnp.where(is_last, 1, 0)]
-        for block in range(4):
-            ahead = rows[:, 128 * block : 128 * block + 128]
-            behind = rows[:, 128 * (3 - block) : 128 * (3 - block) + 128]
+        for block_at in range(4):
+            ahead = rows[:, 128 * block_at : 128 * block_at + 128]
+            behind = rows[:, 128 * (3 - block_at) : 128 * (3 - block_at) + 128]
             w = jnp.where(is_last, behind, ahead)
             e = jnp.where(is_last, ahead, behind)
-            scat_p[block] = jnp.zeros((8, 128), F32)
-            scat_p[block, 0:1, :] = w[5:6]
-            scat_p[block, 1:2, :] = e[4:5]
+            scat_p[block_at] = jnp.zeros((8, 128), F32)
+            scat_p[block_at, 0:1, :] = w[5:6]
+            scat_p[block_at, 1:2, :] = e[4:5]
 
         def one(u, c):
             @pl.when(jnp.logical_and(u != t, is_last))
@@ -495,8 +514,16 @@
         def _():
             hub_in[1] = scat_p[t // 8]
 
-    for p in range(PANELS):
-        part[p] = fold(fold_rows, acc[p, 1:17].reshape(8 * ROWS, CELLS))
+    lax.fori_loop(4, PANELS, inner, 0)
+    lax.fori_loop(3, PANELS, lambda n, c: fold_leaving(n * (n // 4), c), 0)
+    send_mirror(1)
+
+    def fold_part(p, c):
+        mine = acc[p, 1:17] + (acc_s[p, 1:17] - acc_n[p, 1:17])
+        part[p] = fold(fold_rows, mine.reshape(8 * ROWS, CELLS))
+        return c
+
+    lax.fori_loop(0, PANELS, fold_part, 0)
 
     def add_column(p, side, column):
         if side:
@@ -518,7 +545,6 @@
 
     p_south.wait_recv()
     p_north.wait_recv()
-    panel_row = iota((8, CELLS), 0)
     from_north = precv[0]
     from_south = precv[1]
     pad = jnp.zeros((4, CELLS), F32)
@@ -528,10 +554,72 @@
         part[p, 0:1, :] += from_north[p : p + 1]
         part[p, ROWS - 1 : ROWS, :] += from_south[p : p + 1]
 
-    p_mirror.wait_recv()
-    for n in range(4):
-        _, (a, b) = MIRRORED[n]
-        add_column(a, b, row_to_column(mirror_in[n : n + 1, :], 0, False))
+    def from_mirror(m):
+        p_mirror(m).wait_recv()
+        for n in range(2):
+            _, (a, b) = MIRRORED[2 * m + n]
+            add_column(a, b, row_to_column(mirror_in[m, n : n + 1, :], 0, False))
+
+    from_mirror(0)
+
+    @pl.when(is_hub)
+    def _():
+        def wait_one(u, c):
+            @pl.when(u != t)
+            def _():
+                remote(hub_out.at[0], gath_p.at[u], ph_send.at[0], pgath_recv.at[u], {"tile": u}).wait_recv()
+            return c
+
+        lax.fori_loop(0, TILES, wait_one, 0)
+        row_at = jnp.where(is_last, ROWS - 1, 0)
+        for block_at in range(4):
+            cols = slice(128 * block_at, 128 * block_at + 128)
+            for side in range(2):
+                total = jnp.zeros((8, 128), F32)
+                for k in range(8):
+                    seg = 8 * block_at + k
+                    total = total + gath_p[seg_e(seg) if side else seg_w(seg)]
+                row = jnp.broadcast_to(total[side : side + 1, :], (16, 128))
+                part[5 - side, :, cols] += jnp.where(row16 == row_at, row, 0.0)
+
+    GROUPS = ((0, 4, 5), (1, 2, 3))
+
+    def each_peer(fn):
+        def one(d, c):
+            fn((s + d) % SAMPS)
+            return c
+
+        lax.fori_loop(1, SAMPS, one, 0)
+
+    def reduce_to(m, peer):
+        return remote(rs_in.at[m, peer], ag.at[m, s], rs_send.at[m, peer], rs_recv.at[m, s], {"samp": peer})
+
+    def reduce_from(m, peer):
+        return remote(rs_in.at[m, peer], ag.at[m, peer], rs_send.at[m, peer], rs_recv.at[m, peer], {"samp": peer})
+
+    def share_with(m, peer):
+        return remote(done.at[m, s], done.at[m, s], ag_send.at[m, peer], ag_recv.at[m, s], {"samp": peer})
+
+    def share_from(m, peer):
+        return remote(done.at[m, peer], done.at[m, peer], ag_send.at[m, peer], ag_recv.at[m, peer], {"samp": peer})
+
+    def reduce_start(m):
+        for n in range(SAMPS):
+            h, k = n // 4, n % 4
+            for j, p in enumerate(GROUPS[m]):
+                rs_in[m, n, j] = part[p, 8 * h : 8 * h + 8, 128 * k : 128 * k + 128]
+        each_peer(lambda peer: reduce_to(m, peer).start())
+        ag[m, s] = rs_in[m, s]
+
+    def reduce_end(m):
+        each_peer(lambda peer: reduce_from(m, peer).wait_recv())
+        total = ag[m, 0]
+        for n in range(1, SAMPS):
+            total = total + ag[m, n]
+        done[m, s] = total * (0.005 / SAMPS)
+        each_peer(lambda peer: share_with(m, peer).start())
+
+    reduce_start(0)
 
     @pl.when(t != LAST)
     def _():
@@ -545,77 +633,23 @@
     add_column(1, 1, row_to_column(hub_in[0, 1:2, :], 16 * up, False))
     add_column(3, 0, row_to_column(hub_in[1, 0:1, :], 16 * up, False))
     add_column(3, 1, row_to_column(hub_in[1, 1:2, :], 16 * down, True))
-
-    @pl.when(is_hub)
-    def _():
-        def wait_one(u, c):
-            @pl.when(u != t)
-            def _():
-                remote(hub_out.at[0], gath_p.at[u], ph_send.at[0], pgath_recv.at[u], {"tile": u}).wait_recv()
-            return c
-
-        lax.fori_loop(0, TILES, wait_one, 0)
-
-        def hub_row(block, side):
-            total = jnp.zeros((8, 128), F32)
-            for k in range(8):
-                seg = 8 * block + k
-                total = total + gath_p[seg_e(seg) if side else seg_w(seg)]
-            return total[side : side + 1, :]
-
-        for block in range(4):
-            for side in range(2):
-                row = hub_row(block, side)
-                at = 128 * block
-
-                @pl.when(is_last)
-                def _():
-                    part[5 - side, ROWS - 1 : ROWS, at : at + 128] += row
-
-                @pl.when(is_first)
-                def _():
-                    part[5 - side, 0:1, at : at + 128] += row
-
-    for n in range(SAMPS):
-        h, k = n // 4, n % 4
-        rs_in[n] = part[:, 8 * h : 8 * h + 8, 128 * k : 128 * k + 128]
-
-    def each_peer(fn):
-        def one(d, c):
-            fn((s + d) % SAMPS)
-            return c
-
-        lax.fori_loop(1, SAMPS, one, 0)
-
-    def reduce_to(peer):
-        return remote(rs_in.at[peer], ag.at[s], rs_send.at[peer], rs_recv.at[s], {"samp": peer})
-
-    def reduce_from(peer):
-        return remote(rs_in.at[peer], ag.at[peer], rs_send.at[peer], rs_recv.at[peer], {"samp": peer})
-
-    each_peer(lambda peer: reduce_to(peer).start())
-    ag[s] = rs_in[s]
-    each_peer(lambda peer: reduce_from(peer).wait_recv())
-    each_peer(lambda peer: reduce_to(peer).wait_send())
-    total = ag[0]
-    for n in range(1, SAMPS):
-        total = total + ag[n]
-    done[s] = total * (0.005 / SAMPS)
-
-    def share_with(peer):
-        return remote(done.at[s], done.at[s], ag_send.at[peer], ag_recv.at[s], {"samp": peer})
-
-    def share_from(peer):
-        return remote(done.at[peer], done.at[peer], ag_send.at[peer], ag_recv.at[peer], {"samp": peer})
-
-    each_peer(lambda peer: share_with(peer).start())
-    each_peer(lambda peer: share_from(peer).wait_recv())
-    for n in range(SAMPS):
-        h, k = n // 4, n % 4
-        out_ref[:, 8 * h : 8 * h + 8, 128 * k : 128 * k + 128] = done[n]
-
-    each_peer(lambda peer: share_with(peer).wait_send())
-    for p in range(PANELS):
+    from_mirror(1)
+    reduce_start(1)
+    reduce_end(0)
+    reduce_end(1)
+    for m in range(2):
+        each_peer(lambda peer: share_from(m, peer).wait_recv())
+        for n in range(SAMPS):
+            h, k = n // 4, n % 4
+            for j, p in enumerate(GROUPS[m]):
+                out_ref[p, 8 * h : 8 * h + 8, 128 * k : 128 * k + 128] = done[m, n, j]
+
+    for m in range(2):
+        each_peer(lambda peer: reduce_to(m, peer).wait_send())
+        each_peer(lambda peer: share_with(m, peer).wait_send())
+        p_mirror(m).wait_send()
+
+    def rows_left(p, c):
         @pl.when(south_goes(p))
         def _():
             row_south(p).wait_send()
@@ -624,11 +658,13 @@
         def _():
             row_north(p).wait_send()
 
+        return c
+
+    lax.fori_loop(0, PANELS, rows_left, 0)
     for n in range(4):
         mirrored(n).wait_send()
     p_south.wait_send()
     p_north.wait_send()
-    p_mirror.wait_send()
     for hub in (LAST, 0):
         @pl.when(t != hub)
         def _():
@@ -668,33 +704,36 @@
             pltpu.VMEM((PANELS, ROWS + 2, 40, CELLS), F32),
             pltpu.VMEM((PANELS, ROWS, LAYERS, CELLS), F32),
             pltpu.VMEM((PANELS, ROWS + 2, 8, CELLS), F32),
+            pltpu.VMEM((PANELS, ROWS + 2, 8, CELLS), F32),
+            pltpu.VMEM((PANELS, ROWS + 2, 8, CELLS), F32),
             pltpu.VMEM((PANELS, ROWS) + tile, F32),
+            pltpu.VMEM((PANELS, ROWS, 128), F32),
             pltpu.VMEM((PANELS, 2) + tile, F32),
             pltpu.VMEM((PANELS, 2) + tile, F32),
             pltpu.VMEM((TILES, 2) + tile, F32),
             pltpu.VMEM((TILES, 2) + tile, F32),
             pltpu.VMEM((2, 8, CELLS), F32),
             pltpu.VMEM((2, 8, CELLS), F32),
-            pltpu.VMEM(tile, F32),
-            pltpu.VMEM(tile, F32),
+            pltpu.VMEM((2,) + tile, F32),
+            pltpu.VMEM((2,) + tile, F32),
             pltpu.VMEM((2,) + tile, F32),
             pltpu.VMEM((TILES,) + tile, F32),
             pltpu.VMEM((4,) + tile, F32),
             pltpu.VMEM((2,) + tile, F32),
             pltpu.VMEM((PANELS, ROWS, CELLS), F32),
-            pltpu.VMEM((SAMPS, PANELS) + tile, F32),
-            pltpu.VMEM((SAMPS, PANELS) + tile, F32),
-            pltpu.VMEM((SAMPS, PANELS) + tile, F32),
+            pltpu.VMEM((2, SAMPS, 3) + tile, F32),
+            pltpu.VMEM((2, SAMPS, 3) + tile, F32),
+            pltpu.VMEM((2, SAMPS, 3) + tile, F32),
             dma((PANELS,)), dma((PANELS,)), dma((2,)),
             dma((2, PANELS)), dma((2, PANELS)),
             dma((2,)), dma((TILES,)), dma((4,)), dma((4,)),
             dma((TILES,)), dma((2,)),
-            dma((2,)), dma((2,)), dma((1,)), dma((1,)),
+            dma((2,)), dma((2,)), dma((2,)), dma((2,)),
             dma((2,)), dma((TILES,)), dma((TILES,)), dma((2,)),
-            dma((SAMPS,)), dma((SAMPS,)), dma((SAMPS,)), dma((SAMPS,)),
+            dma((2, SAMPS)), dma((2, SAMPS)), dma((2, SAMPS)), dma((2, SAMPS)),
         ],
         compiler_params=pltpu.CompilerParams(
-            collective_id=0, has_side_effects=True, vmem_limit_bytes=48 * 1024 * 1024
+            collective_id=0, has_side_effects=True, vmem_limit_bytes=56 * 1024 * 1024
         ),
         cost_estimate=pl.CostEstimate(flops=200_000_000, bytes_accessed=7_000_000, transcendentals=0),
     )(bathymetry, initial_state, patterns, pattern_index, coupling, final_weights)

time: 58.7 us -> 55.6 us (0.947)
  local copies, waits for them, and re-layouts: 5.84 us -> 1.62 us
  Pallas kernels: 52.6 us -> 53.7 us
    unnamed x11 -> x1, local copies, waits for them, and re-layouts: 5.84 us -> 1.62 us
    pallas_call x1, Pallas kernels: 52.6 us -> 53.7 us  [body(): pl.pallas_call(kernel, out_shape=jax.ShapeDtypeStruct((PANELS, ROWS, CELL...]
where the time goes in v2:
time: 55.6 us; the launch traced here: 55.3 us
  Pallas kernels  53.7 us (97%)
  local copies, waits for them, and re-layouts  1.62 us (3%)
    pallas_call x1, Pallas kernels, body(): pl.pallas_call(kernel, out_shape=jax.ShapeDtypeStruct((PANELS, ROWS, CELL...  53.7 us
    unnamed x1, local copies, waits for them, and re-layouts  1.62 us

profile of v2, /device:TPU:4, one launch (start us, length us, event | category | flops | bytes accessed | tf_op | source)
XLA Modules:
  0.0 55.3 jit_solution(17248972319832140522)
XLA Ops:
  0.0 53.7 %shard_map.64 = f32[6,16,512]{2,1,0:T(8,128)} custom-call(f32[6,16,512]{2,1,0:T(8,128)} %depth_hbm.1, f32[16,6,16,512]{3,2,1,0:T(8,128)} %state_hbm.1, bf16[4,6,16,512]{3,2,1,0:T(8,128)(2,1)} %pattern_hbm.1, s32[1,16]{1,0:T(1,128)} %index_ref.1, f32[16,16]{1,0:T(8,128)} %coupling_ref.1, f32[1,16,6,16,512]{4,3,2,1,0:T(8,128)} %weight_hbm.1), custom_call_target="tpu_custom_call" | custom-call | flops 200000000 | bytes 7000000 | tf_op jit(solution)/shard_map/pallas_call | solution.py:691
  53.7 1.6 %copy.8 = f32[6,16,512]{2,1,0:T(8,128)} copy(f32[6,16,512]{2,1,0:T(8,128)} %shard_map.64) | data formatting | bytes 393216

commit v3 on v2

--- a/solution.py
+++ b/solution.py
@@ -26,7 +26,7 @@
 
 def kernel(
     depth_hbm, state_hbm, pattern_hbm, index_ref, coupling_ref, weight_hbm, out_ref,
-    xs, ws, ps, bs, kz, kv, kq, field, qf, acc, acc_s, acc_n, ocs, leaving, pk, colh, gath, scat, prow, precv,
+    xs, ws, ps, bs, kz, kv, kq, field, qf, acc_e, acc_w, acc_s, acc_n, sum_e, sum_w, pk, colh, gath, scat, prow, precv,
     mirror_out, mirror_in, hub_out, gath_p, scat_p, hub_in, part, rs_in, ag, done,
     load_x, load_w, load_pb, row_send, row_recv, hub_send, gath_recv, mir_send, mir_recv,
     scat_send, scat_recv, p_send, p_recv, pm_send, pm_recv, ph_send, pgath_recv, ps_send, ps_recv,
@@ -269,48 +269,31 @@
     def stencil_row(p, i):
         slot = i + 1
         west, east = colh[p, 0], colh[p, 1]
-        at = {}
-
-        def here(g, k):
-            if (g, k) not in at:
-                x = block(g, p, slot, k)
-                at[g, k] = x, pltpu.roll(x, 127, 1)
-            return at[g, k]
-
-        def east_of(g, k):
-            x, turned = here(g, k)
-            if k < 3:
-                after = here(g, k + 1)[1]
-            else:
-                after = pltpu.roll(east, (127 - 16 * g - i) % 128, 1)
-            return x, jnp.where(last_lane, after, turned)
-
-        before = {}
-
-        def west_of(g, k, value, x):
-            turned = pltpu.roll(value, 1, 1)
-            if k == 0:
-                edge = pltpu.roll(west, (128 - 16 * g - i) % 128, 1)
-                edge = x + edge if g == 4 else x - edge
-            else:
-                edge = before[g]
-            before[g] = turned
-            return jnp.where(first_lane, edge, turned)
-
-        held = {}
+
+        def sides(g):
+            x = [block(g, p, slot, k) for k in range(4)]
+            r = [pltpu.roll(y, 127, 1) for y in x] + [pltpu.roll(east, (127 - 16 * g - i) % 128, 1)]
+            l = [pltpu.roll(west, (128 - 16 * g - i) % 128, 1)] + [pltpu.roll(y, 1, 1) for y in x]
+            return (
+                x,
+                [jnp.where(last_lane, r[k + 1], r[k]) for k in range(4)],
+                [jnp.where(first_lane, l[k], l[k + 1]) for k in range(4)],
+            )
+
+        every = [sides(g) for g in range(5)]
         for k in range(4):
-            x, e = east_of(4, k)
+            x, e, w = (v[k] for v in every[4])
             beta_e = x + e
-            beta_w = west_of(4, k, beta_e, x)
+            beta_w = x + w
             beta_s = x + block(4, p, slot + 1, k)
             beta_n = x + block(4, p, slot - 1, k)
             sums = None
             for half in range(2):
                 both = []
                 for g in (half, 2 + half):
-                    x, e = east_of(g, k)
+                    x, e, w = (v[k] for v in every[g])
                     de = e - x
-                    dw = west_of(g, k, de, x)
+                    dw = x - w
                     ds = block(g, p, slot + 1, k) - x
                     dn = x - block(g, p, slot - 1, k)
                     lap = (beta_e * de - beta_w * dw) + (beta_s * ds - beta_n * dn)
@@ -319,23 +302,11 @@
                 q = lz + qf[p, i, 8 * half : 8 * half + 8, 128 * k : 128 * k + 128]
                 terms = [x * q + y * lv for x, y in zip(dv, dz)]
                 sums = terms if sums is None else [x + y for x, y in zip(sums, terms)]
-            pe, pw, p_s, p_n = sums
             cols = slice(128 * k, 128 * k + 128)
-            acc_s[p, slot + 1, :, cols] = p_s
-            acc_n[p, slot - 1, :, cols] = p_n
-            own = (pe + p_s) - (pw + p_n)
-            pe_turned = pltpu.roll(pe, 1, 1)
-            own = own + jnp.where(first_lane, held["e"] if k else 0.0, pe_turned)
-            pw_turned = pltpu.roll(pw, 127, 1)
-            if k == 0:
-                first = pw_turned
-            else:
-                acc[p, slot, :, 128 * k - 128 : 128 * k] = held["own"] - jnp.where(
-                    last_lane, pw_turned, held["w"]
-                )
-            held = {"e": pe_turned, "w": pw_turned, "own": own}
-        acc[p, slot, :, 384:512] = held["own"] - jnp.where(last_lane, 0.0, held["w"])
-        ocs[p, i] = jnp.where(first_lane, held["e"], jnp.where(last_lane, -first, 0.0))
+            acc_e[p, i, :, cols] = sums[0]
+            acc_w[p, i, :, cols] = sums[1]
+            acc_s[p, slot + 1, :, cols] = sums[2]
+            acc_n[p, slot - 1, :, cols] = sums[3]
 
     def stencil_rows(p, start, count):
         for r in range(count):
@@ -368,11 +339,11 @@
         def _():
             wait_columns()
 
-        def two(n, c):
-            stencil_rows(p, 1 + 2 * n, 2)
+        def seven(n, c):
+            stencil_rows(p, 1 + 7 * n, 7)
             return c
 
-        lax.fori_loop(0, 7, two, 0)
+        lax.fori_loop(0, 2, seven, 0)
         return c
 
     lax.fori_loop(0, 4, inner, 0)
@@ -433,13 +404,14 @@
     p_north.start()
 
     def fold_leaving(p, c):
-        leaving[p] = fold(fold_rows, ocs[p].reshape(8 * ROWS, 128))
+        sum_e[p] = fold(fold_rows, acc_e[p].reshape(8 * ROWS, CELLS))
+        sum_w[p] = fold(fold_rows, acc_w[p].reshape(8 * ROWS, CELLS))
         return c
 
     lax.fori_loop(1, 4, fold_leaving, 0)
 
     def leaving_column(p, side):
-        return leaving[p][:, 0:1] if side else leaving[p][:, 127:128]
+        return sum_e[p, :, CELLS - 128 :][:, 127:128] if side else -sum_w[p, :, 0:128][:, 0:1]
 
     def leaving_row(p, side, reverse):
         spot = 15 - row16 if reverse else row16
@@ -518,9 +490,14 @@
     lax.fori_loop(3, PANELS, lambda n, c: fold_leaving(n * (n // 4), c), 0)
     send_mirror(1)
 
+    cell = iota((ROWS, CELLS), 1)
+
     def fold_part(p, c):
-        mine = acc[p, 1:17] + (acc_s[p, 1:17] - acc_n[p, 1:17])
-        part[p] = fold(fold_rows, mine.reshape(8 * ROWS, CELLS))
+        mine = (acc_s[p, 2:18] + acc_s[p, 1:17]) - (acc_n[p, 0:16] + acc_n[p, 1:17])
+        to_e, to_w = sum_e[p], sum_w[p]
+        moved_e = jnp.where(cell == 0, 0.0, pltpu.roll(to_e, 1, 1))
+        moved_w = jnp.where(cell == CELLS - 1, 0.0, pltpu.roll(to_w, CELLS - 1, 1))
+        part[p] = fold(fold_rows, mine.reshape(8 * ROWS, CELLS)) + ((to_e - to_w) + (moved_e - moved_w))
         return c
 
     lax.fori_loop(0, PANELS, fold_part, 0)
@@ -703,11 +680,12 @@
             pltpu.VMEM((256, 576), BF16),
             pltpu.VMEM((PANELS, ROWS + 2, 40, CELLS), F32),
             pltpu.VMEM((PANELS, ROWS, LAYERS, CELLS), F32),
+            pltpu.VMEM((PANELS, ROWS, 8, CELLS), F32),
+            pltpu.VMEM((PANELS, ROWS, 8, CELLS), F32),
             pltpu.VMEM((PANELS, ROWS + 2, 8, CELLS), F32),
             pltpu.VMEM((PANELS, ROWS + 2, 8, CELLS), F32),
-            pltpu.VMEM((PANELS, ROWS + 2, 8, CELLS), F32),
-            pltpu.VMEM((PANELS, ROWS) + tile, F32),
-            pltpu.VMEM((PANELS, ROWS, 128), F32),
+            pltpu.VMEM((PANELS, ROWS, CELLS), F32),
+            pltpu.VMEM((PANELS, ROWS, CELLS), F32),
             pltpu.VMEM((PANELS, 2) + tile, F32),
             pltpu.VMEM((PANELS, 2) + tile, F32),
             pltpu.VMEM((TILES, 2) + tile, F32),

time: 55.6 us -> 50.7 us (0.912)
  Pallas kernels: 53.7 us -> 49 us
    pallas_call x1, Pallas kernels: 53.7 us -> 49 us  [body(): pl.pallas_call(kernel, out_shape=jax.ShapeDtypeStruct((PANELS, ROWS, CELL...]
where the time goes in v3:
time: 50.7 us; the launch traced here: 50.6 us
  Pallas kernels  49 us (97%)
  local copies, waits for them, and re-layouts  1.62 us (3%)
    pallas_call x1, Pallas kernels, body(): pl.pallas_call(kernel, out_shape=jax.ShapeDtypeStruct((PANELS, ROWS, CELL...  49 us
    unnamed x1, local copies, waits for them, and re-layouts  1.62 us

profile of v3, /device:TPU:4, one launch (start us, length us, event | category | flops | bytes accessed | tf_op | source)
XLA Modules:
  0.0 50.6 jit_solution(10400170209260420627)
XLA Ops:
  0.0 49.0 %shard_map.64 = f32[6,16,512]{2,1,0:T(8,128)} custom-call(f32[6,16,512]{2,1,0:T(8,128)} %depth_hbm.1, f32[16,6,16,512]{3,2,1,0:T(8,128)} %state_hbm.1, bf16[4,6,16,512]{3,2,1,0:T(8,128)(2,1)} %pattern_hbm.1, s32[1,16]{1,0:T(1,128)} %index_ref.1, f32[16,16]{1,0:T(8,128)} %coupling_ref.1, f32[1,16,6,16,512]{4,3,2,1,0:T(8,128)} %weight_hbm.1), custom_call_target="tpu_custom_call" | custom-call | flops 200000000 | bytes 7000000 | tf_op jit(solution)/shard_map/pallas_call | solution.py:668
  49.0 1.6 %copy.8 = f32[6,16,512]{2,1,0:T(8,128)} copy(f32[6,16,512]{2,1,0:T(8,128)} %shard_map.64) | data formatting | bytes 393216

commit v4 on v3

--- a/solution.py
+++ b/solution.py
@@ -27,7 +27,7 @@
 def kernel(
     depth_hbm, state_hbm, pattern_hbm, index_ref, coupling_ref, weight_hbm, out_ref,
     xs, ws, ps, bs, kz, kv, kq, field, qf, acc_e, acc_w, acc_s, acc_n, sum_e, sum_w, pk, colh, gath, scat, prow, precv,
-    mirror_out, mirror_in, hub_out, gath_p, scat_p, hub_in, part, rs_in, ag, done,
+    mirror_out, mirror_in, hub_out, gath_p, scat_p, hub_in, part, rs_in, ag, done, late_in, late_ag, late_done, direct,
     load_x, load_w, load_pb, row_send, row_recv, hub_send, gath_recv, mir_send, mir_recv,
     scat_send, scat_recv, p_send, p_recv, pm_send, pm_recv, ph_send, pgath_recv, ps_send, ps_recv,
     rs_send, rs_recv, ag_send, ag_recv,
@@ -245,7 +245,7 @@
         def _():
             make_scatter()
 
-        @pl.when(step == 5)
+        @pl.when(step == 3)
         def _():
             for n in range(4):
                 mirrored(n).start()
@@ -408,7 +408,7 @@
         sum_w[p] = fold(fold_rows, acc_w[p].reshape(8 * ROWS, CELLS))
         return c
 
-    lax.fori_loop(1, 4, fold_leaving, 0)
+    lax.fori_loop(0, 4, fold_leaving, 0)
 
     def leaving_column(p, side):
         return sum_e[p, :, CELLS - 128 :][:, 127:128] if side else -sum_w[p, :, 0:128][:, 0:1]
@@ -486,9 +486,64 @@
         def _():
             hub_in[1] = scat_p[t // 8]
 
-    lax.fori_loop(4, PANELS, inner, 0)
-    lax.fori_loop(3, PANELS, lambda n, c: fold_leaving(n * (n // 4), c), 0)
-    send_mirror(1)
+    GROUPS = ((0, 1, 2, 3),)
+
+    def each_peer(fn):
+        def one(d, c):
+            fn((s + d) % SAMPS)
+            return c
+
+        lax.fori_loop(1, SAMPS, one, 0)
+
+    def reduce_to(m, peer):
+        return remote(rs_in.at[m, peer], ag.at[m, s], rs_send.at[m, peer], rs_recv.at[m, s], {"samp": peer})
+
+    def reduce_from(m, peer):
+        return remote(rs_in.at[m, peer], ag.at[m, peer], rs_send.at[m, peer], rs_recv.at[m, peer], {"samp": peer})
+
+    def share_with(m, peer):
+        return remote(done.at[m, s], done.at[m, s], ag_send.at[m, peer], ag_recv.at[m, s], {"samp": peer})
+
+    def share_from(m, peer):
+        return remote(done.at[m, peer], done.at[m, peer], ag_send.at[m, peer], ag_recv.at[m, peer], {"samp": peer})
+
+    def direct_to(peer):
+        return remote(part.at[pl.ds(4, 2)], direct.at[s], rs_send.at[1, peer], rs_recv.at[1, s], {"samp": peer})
+
+    def direct_from(peer):
+        return remote(part.at[pl.ds(4, 2)], direct.at[peer], rs_send.at[1, peer], rs_recv.at[1, peer], {"samp": peer})
+
+    def late_to(peer):
+        return remote(late_in, late_ag.at[s], rs_send.at[2, peer], rs_recv.at[2, s], {"samp": peer})
+
+    def late_from(peer):
+        return remote(late_in, late_ag.at[peer], rs_send.at[2, peer], rs_recv.at[2, peer], {"samp": peer})
+
+    def summed(parts):
+        total = parts[0]
+        for n in range(1, SAMPS):
+            total = total + parts[n]
+        return total * (0.005 / SAMPS)
+
+    def reduce_start(m):
+        for n in range(SAMPS):
+            h, k = n // 4, n % 4
+            for j, p in enumerate(GROUPS[m]):
+                rs_in[m, n, j] = part[p, 8 * h : 8 * h + 8, 128 * k : 128 * k + 128]
+        each_peer(lambda peer: reduce_to(m, peer).start())
+        ag[m, s] = rs_in[m, s]
+
+    def reduce_end(m):
+        each_peer(lambda peer: reduce_from(m, peer).wait_recv())
+        done[m, s] = summed([ag[m, n] for n in range(SAMPS)])
+        each_peer(lambda peer: share_with(m, peer).start())
+
+    def share_end(m):
+        each_peer(lambda peer: share_from(m, peer).wait_recv())
+        for n in range(SAMPS):
+            h, k = n // 4, n % 4
+            for j, p in enumerate(GROUPS[m]):
+                out_ref[p, 8 * h : 8 * h + 8, 128 * k : 128 * k + 128] = done[m, n, j]
 
     cell = iota((ROWS, CELLS), 1)
 
@@ -500,25 +555,32 @@
         part[p] = fold(fold_rows, mine.reshape(8 * ROWS, CELLS)) + ((to_e - to_w) + (moved_e - moved_w))
         return c
 
-    lax.fori_loop(0, PANELS, fold_part, 0)
-
-    def add_column(p, side, column):
-        if side:
-            at, lane = CELLS - 128, 127
-        else:
-            at, lane = 0, 0
+    lax.fori_loop(0, 4, fold_part, 0)
+    reduce_start(0)
+
+    lax.fori_loop(4, PANELS, inner, 0)
+    lax.fori_loop(4, PANELS, fold_leaving, 0)
+    send_mirror(1)
+    lax.fori_loop(4, PANELS, fold_part, 0)
+
+    def add_column(target, p, side, column):
+        at, lane = (CELLS - 128, 127) if side else (0, 0)
         spread_out = jnp.broadcast_to(column, (16, 128))
-        part[p, :, at : at + 128] += jnp.where(lane16 == lane, spread_out, 0.0)
-
-    add_column(5, 1, leaving_column(0, 0))
-    add_column(4, 0, leaving_column(0, 1))
-    add_column(0, 1, leaving_column(4, 0))
-    add_column(0, 0, leaving_column(5, 1))
+        target[p, :, at : at + 128] += jnp.where(lane16 == lane, spread_out, 0.0)
+
+    add_column(part, 5, 1, leaving_column(0, 0))
+    add_column(part, 4, 0, leaving_column(0, 1))
+    each_peer(lambda peer: direct_to(peer).start())
+    direct[s] = part[4:6]
+    reduce_end(0)
 
     def row_to_column(row, base, reverse):
         spot = base + (15 - row16 if reverse else row16)
         spread_out = jnp.broadcast_to(row, (16, 128))
         return jnp.sum(jnp.where(lane16 == spot, spread_out, 0.0), axis=1, keepdims=True)
+
+    def placed(p, side, column):
+        return jnp.where(lane16 == 2 * p + side, jnp.broadcast_to(column, (16, 128)), 0.0)
 
     p_south.wait_recv()
     p_north.wait_recv()
@@ -527,17 +589,9 @@
     pad = jnp.zeros((4, CELLS), F32)
     from_north = jnp.where(is_first, jnp.concatenate([from_north[3:4], from_north[0:3], pad], 0), from_north)
     from_south = jnp.where(is_last, jnp.concatenate([from_south[1:4], from_south[0:1], pad], 0), from_south)
-    for p in range(PANELS):
-        part[p, 0:1, :] += from_north[p : p + 1]
-        part[p, ROWS - 1 : ROWS, :] += from_south[p : p + 1]
-
-    def from_mirror(m):
-        p_mirror(m).wait_recv()
-        for n in range(2):
-            _, (a, b) = MIRRORED[2 * m + n]
-            add_column(a, b, row_to_column(mirror_in[m, n : n + 1, :], 0, False))
-
-    from_mirror(0)
+    for n in range(SAMPS):
+        h, k = n // 4, n % 4
+        late_in[n] = (from_south if h else from_north)[:, 128 * k : 128 * k + 128]
 
     @pl.when(is_hub)
     def _():
@@ -548,55 +602,16 @@
             return c
 
         lax.fori_loop(0, TILES, wait_one, 0)
-        row_at = jnp.where(is_last, ROWS - 1, 0)
+        panel_row = iota((8, 128), 0)
+        first_chunk = 4 * at_end
         for block_at in range(4):
-            cols = slice(128 * block_at, 128 * block_at + 128)
             for side in range(2):
                 total = jnp.zeros((8, 128), F32)
                 for k in range(8):
                     seg = 8 * block_at + k
                     total = total + gath_p[seg_e(seg) if side else seg_w(seg)]
-                row = jnp.broadcast_to(total[side : side + 1, :], (16, 128))
-                part[5 - side, :, cols] += jnp.where(row16 == row_at, row, 0.0)
-
-    GROUPS = ((0, 4, 5), (1, 2, 3))
-
-    def each_peer(fn):
-        def one(d, c):
-            fn((s + d) % SAMPS)
-            return c
-
-        lax.fori_loop(1, SAMPS, one, 0)
-
-    def reduce_to(m, peer):
-        return remote(rs_in.at[m, peer], ag.at[m, s], rs_send.at[m, peer], rs_recv.at[m, s], {"samp": peer})
-
-    def reduce_from(m, peer):
-        return remote(rs_in.at[m, peer], ag.at[m, peer], rs_send.at[m, peer], rs_recv.at[m, peer], {"samp": peer})
-
-    def share_with(m, peer):
-        return remote(done.at[m, s], done.at[m, s], ag_send.at[m, peer], ag_recv.at[m, s], {"samp": peer})
-
-    def share_from(m, peer):
-        return remote(done.at[m, peer], done.at[m, peer], ag_send.at[m, peer], ag_recv.at[m, peer], {"samp": peer})
-
-    def reduce_start(m):
-        for n in range(SAMPS):
-            h, k = n // 4, n % 4
-            for j, p in enumerate(GROUPS[m]):
-                rs_in[m, n, j] = part[p, 8 * h : 8 * h + 8, 128 * k : 128 * k + 128]
-        each_peer(lambda peer: reduce_to(m, peer).start())
-        ag[m, s] = rs_in[m, s]
-
-    def reduce_end(m):
-        each_peer(lambda peer: reduce_from(m, peer).wait_recv())
-        total = ag[m, 0]
-        for n in range(1, SAMPS):
-            total = total + ag[m, n]
-        done[m, s] = total * (0.005 / SAMPS)
-        each_peer(lambda peer: share_with(m, peer).start())
-
-    reduce_start(0)
+                row = jnp.broadcast_to(total[side : side + 1, :], (8, 128))
+                late_in[first_chunk + block_at] += jnp.where(panel_row == 5 - side, row, 0.0)
 
     @pl.when(t != LAST)
     def _():
@@ -606,25 +621,38 @@
     def _():
         scatter_p(0, 0).wait_recv()
 
-    add_column(1, 0, row_to_column(hub_in[0, 0:1, :], 16 * down, True))
-    add_column(1, 1, row_to_column(hub_in[0, 1:2, :], 16 * up, False))
-    add_column(3, 0, row_to_column(hub_in[1, 0:1, :], 16 * up, False))
-    add_column(3, 1, row_to_column(hub_in[1, 1:2, :], 16 * down, True))
-    from_mirror(1)
-    reduce_start(1)
-    reduce_end(0)
-    reduce_end(1)
+    columns = placed(0, 1, leaving_column(4, 0)) + placed(0, 0, leaving_column(5, 1))
+    columns = columns + placed(1, 0, row_to_column(hub_in[0, 0:1, :], 16 * down, True))
+    columns = columns + placed(1, 1, row_to_column(hub_in[0, 1:2, :], 16 * up, False))
+    columns = columns + placed(3, 0, row_to_column(hub_in[1, 0:1, :], 16 * up, False))
+    columns = columns + placed(3, 1, row_to_column(hub_in[1, 1:2, :], 16 * down, True))
     for m in range(2):
-        each_peer(lambda peer: share_from(m, peer).wait_recv())
-        for n in range(SAMPS):
-            h, k = n // 4, n % 4
-            for j, p in enumerate(GROUPS[m]):
-                out_ref[p, 8 * h : 8 * h + 8, 128 * k : 128 * k + 128] = done[m, n, j]
-
-    for m in range(2):
-        each_peer(lambda peer: reduce_to(m, peer).wait_send())
-        each_peer(lambda peer: share_with(m, peer).wait_send())
-        p_mirror(m).wait_send()
+        p_mirror(m).wait_recv()
+        for n in range(2):
+            _, (a, b) = MIRRORED[2 * m + n]
+            columns = columns + placed(a, b, row_to_column(mirror_in[m, n : n + 1, :], 0, False))
+    late_in[8] = columns[0:8]
+    late_in[9] = columns[8:16]
+    each_peer(lambda peer: late_to(peer).start())
+    late_ag[s] = late_in[...]
+    each_peer(lambda peer: direct_from(peer).wait_recv())
+    out_ref[4:6] = summed([direct[n] for n in range(SAMPS)])
+    share_end(0)
+    each_peer(lambda peer: late_from(peer).wait_recv())
+    late_done[...] = summed([late_ag[n] for n in range(SAMPS)])
+    for n in range(SAMPS):
+        h, k = n // 4, n % 4
+        for p in range(PANELS):
+            row = slice(15, 16) if h else slice(0, 1)
+            out_ref[p, row, 128 * k : 128 * k + 128] += late_done[n, p : p + 1, :]
+    columns = jnp.concatenate([late_done[8], late_done[9]], 0)
+    for p, side in ((0, 0), (0, 1), (1, 0), (1, 1), (3, 0), (3, 1), (2, 0), (2, 1), (5, 0), (4, 1)):
+        add_column(out_ref, p, side, columns[:, 2 * p + side : 2 * p + side + 1])
+
+    for copy_to in (lambda peer: reduce_to(0, peer), lambda peer: share_with(0, peer), direct_to, late_to):
+        each_peer(lambda peer: copy_to(peer).wait_send())
+    p_mirror(0).wait_send()
+    p_mirror(1).wait_send()
 
     def rows_left(p, c):
         @pl.when(south_goes(p))
@@ -699,16 +727,20 @@
             pltpu.VMEM((4,) + tile, F32),
             pltpu.VMEM((2,) + tile, F32),
             pltpu.VMEM((PANELS, ROWS, CELLS), F32),
-            pltpu.VMEM((2, SAMPS, 3) + tile, F32),
-            pltpu.VMEM((2, SAMPS, 3) + tile, F32),
-            pltpu.VMEM((2, SAMPS, 3) + tile, F32),
+            pltpu.VMEM((1, SAMPS, 4) + tile, F32),
+            pltpu.VMEM((1, SAMPS, 4) + tile, F32),
+            pltpu.VMEM((1, SAMPS, 4) + tile, F32),
+            pltpu.VMEM((10,) + tile, F32),
+            pltpu.VMEM((SAMPS, 10) + tile, F32),
+            pltpu.VMEM((10,) + tile, F32),
+            pltpu.VMEM((SAMPS, 2, ROWS, CELLS), F32),
             dma((PANELS,)), dma((PANELS,)), dma((2,)),
             dma((2, PANELS)), dma((2, PANELS)),
             dma((2,)), dma((TILES,)), dma((4,)), dma((4,)),
             dma((TILES,)), dma((2,)),
             dma((2,)), dma((2,)), dma((2,)), dma((2,)),
             dma((2,)), dma((TILES,)), dma((TILES,)), dma((2,)),
-            dma((2, SAMPS)), dma((2, SAMPS)), dma((2, SAMPS)), dma((2, SAMPS)),
+            dma((3, SAMPS)), dma((3, SAMPS)), dma((1, SAMPS)), dma((1, SAMPS)),
         ],
         compiler_params=pltpu.CompilerParams(
             collective_id=0, has_side_effects=True, vmem_limit_bytes=56 * 1024 * 1024

time: 50.7 us -> 47.6 us (0.939)
  Pallas kernels: 49 us -> 45.6 us
    pallas_call x1, Pallas kernels: 49 us -> 45.6 us  [body(): pl.pallas_call(kernel, out_shape=jax.ShapeDtypeStruct((PANELS, ROWS, CELL...]
where the time goes in v4:
time: 47.6 us; the launch traced here: 47.2 us
  Pallas kernels  45.6 us (96%)
  local copies, waits for them, and re-layouts  1.62 us (3%)
    pallas_call x1, Pallas kernels, body(): pl.pallas_call(kernel, out_shape=jax.ShapeDtypeStruct((PANELS, ROWS, CELL...  45.6 us
    unnamed x1, local copies, waits for them, and re-layouts  1.62 us

profile of v4, /device:TPU:4, one launch (start us, length us, event | category | flops | bytes accessed | tf_op | source)
XLA Modules:
  0.0 47.2 jit_solution(9752299610834050886)
XLA Ops:
  0.0 45.6 %shard_map.64 = f32[6,16,512]{2,1,0:T(8,128)} custom-call(f32[6,16,512]{2,1,0:T(8,128)} %depth_hbm.1, f32[16,6,16,512]{3,2,1,0:T(8,128)} %state_hbm.1, bf16[4,6,16,512]{3,2,1,0:T(8,128)(2,1)} %pattern_hbm.1, s32[1,16]{1,0:T(1,128)} %index_ref.1, f32[16,16]{1,0:T(8,128)} %coupling_ref.1, f32[1,16,6,16,512]{4,3,2,1,0:T(8,128)} %weight_hbm.1), custom_call_target="tpu_custom_call" | custom-call | flops 200000000 | bytes 7000000 | tf_op jit(solution)/shard_map/pallas_call | solution.py:696
  45.6 1.6 %copy.8 = f32[6,16,512]{2,1,0:T(8,128)} copy(f32[6,16,512]{2,1,0:T(8,128)} %shard_map.64) | data formatting | bytes 393216

commit v5 on v4

--- a/solution.py
+++ b/solution.py
@@ -25,7 +25,8 @@
 
 
 def kernel(
-    depth_hbm, state_hbm, pattern_hbm, index_ref, coupling_ref, weight_hbm, out_ref,
+    depth_hbm, state_hbm, pattern_hbm, index_hbm, coupling_hbm, weight_hbm, out_ref,
+    index_ref, coupling_ref,
     xs, ws, ps, bs, kz, kv, kq, field, qf, acc_e, acc_w, acc_s, acc_n, sum_e, sum_w, pk, colh, gath, scat, prow, precv,
     mirror_out, mirror_in, hub_out, gath_p, scat_p, hub_in, part, rs_in, ag, done, late_in, late_ag, late_done, direct,
     load_x, load_w, load_pb, row_send, row_recv, hub_send, gath_recv, mir_send, mir_recv,
@@ -48,6 +49,10 @@
 
     load_p = pltpu.make_async_copy(pattern_hbm, ps, load_pb.at[0])
     load_b = pltpu.make_async_copy(depth_hbm, bs, load_pb.at[1])
+    load_i = pltpu.make_async_copy(index_hbm, index_ref, load_pb.at[2])
+    load_c = pltpu.make_async_copy(coupling_hbm, coupling_ref, load_pb.at[3])
+    load_c.start()
+    load_i.start()
     for step in range(PANELS):
         for copy in load(PANELS - 1 - step):
             copy.start()
@@ -60,22 +65,13 @@
     def greet(device):
         pl.semaphore_signal(barrier, inc=1, device_id=device, device_id_type=MESH)
 
-    def tell_tile(u, c):
-        @pl.when(u != t)
-        def _():
-            greet({"tile": u})
-        return c
-
-    lax.fori_loop(0, TILES, tell_tile, 0)
-
-    def tell_samp(u, c):
-        @pl.when(u != s)
-        def _():
-            greet({"samp": u})
-        return c
-
-    lax.fori_loop(0, SAMPS, tell_samp, 0)
-
+    for d in range(1, SAMPS):
+        greet({"samp": (s + d) % SAMPS})
+    for d in range(1, TILES):
+        greet({"tile": (t + d) % TILES})
+
+    load_c.wait()
+    load_i.wait()
     mixing = coupling_ref[...] + jnp.where(iota((16, 16), 0) == iota((16, 16), 1), 1.0, 0.0)
     to_layer = (iota((256, 16), 0) % 16 == iota((256, 16), 1)).astype(BF16)
     from_layer = (iota((16, 256), 0) == iota((16, 256), 1) // 16).astype(BF16)
@@ -559,8 +555,11 @@
     reduce_start(0)
 
     lax.fori_loop(4, PANELS, inner, 0)
-    lax.fori_loop(4, PANELS, fold_leaving, 0)
+    sum_w[5] = fold(fold_rows, acc_w[5].reshape(8 * ROWS, CELLS))
+    sum_e[4] = fold(fold_rows, acc_e[4].reshape(8 * ROWS, CELLS))
     send_mirror(1)
+    sum_w[4] = fold(fold_rows, acc_w[4].reshape(8 * ROWS, CELLS))
+    sum_e[5] = fold(fold_rows, acc_e[5].reshape(8 * ROWS, CELLS))
     lax.fori_loop(4, PANELS, fold_part, 0)
 
     def add_column(target, p, side, column):
@@ -696,9 +695,11 @@
     return pl.pallas_call(
         kernel,
         out_shape=jax.ShapeDtypeStruct((PANELS, ROWS, CELLS), F32),
-        in_specs=[hbm, hbm, hbm, vmem, vmem, hbm],
+        in_specs=[hbm] * 6,
         out_specs=vmem,
         scratch_shapes=[
+            pltpu.VMEM((1, 16), jnp.int32),
+            pltpu.VMEM((16, 16), F32),
             pltpu.VMEM((PANELS, LAYERS, ROWS, CELLS), F32),
             pltpu.VMEM((PANELS, LAYERS, ROWS, CELLS), F32),
             pltpu.VMEM((4, PANELS, ROWS, CELLS), BF16),
@@ -734,7 +735,7 @@
             pltpu.VMEM((SAMPS, 10) + tile, F32),
             pltpu.VMEM((10,) + tile, F32),
             pltpu.VMEM((SAMPS, 2, ROWS, CELLS), F32),
-            dma((PANELS,)), dma((PANELS,)), dma((2,)),
+            dma((PANELS,)), dma((PANELS,)), dma((4,)),
             dma((2, PANELS)), dma((2, PANELS)),
             dma((2,)), dma((TILES,)), dma((4,)), dma((4,)),
             dma((TILES,)), dma((2,)),

time: 47.6 us -> 47.1 us (0.989)
  no operation moved by 1% of the time
where the time goes in v5:
time: 47.1 us; the launch traced here: 46.8 us
  Pallas kernels  45.2 us (96%)
  local copies, waits for them, and re-layouts  1.62 us (3%)
    pallas_call x1, Pallas kernels, body(): pl.pallas_call(kernel, out_shape=jax.ShapeDtypeStruct((PANELS, ROWS, CELL...  45.2 us
    unnamed x1, local copies, waits for them, and re-layouts  1.62 us

profile of v5, /device:TPU:4, one launch (start us, length us, event | category | flops | bytes accessed | tf_op | source)
XLA Modules:
  0.0 46.8 jit_solution(1065113812177433721)
XLA Ops:
  0.0 45.2 %shard_map.64 = f32[6,16,512]{2,1,0:T(8,128)} custom-call(f32[6,16,512]{2,1,0:T(8,128)} %depth_hbm.1, f32[16,6,16,512]{3,2,1,0:T(8,128)} %state_hbm.1, bf16[4,6,16,512]{3,2,1,0:T(8,128)(2,1)} %pattern_hbm.1, s32[1,16]{1,0:T(1,128)} %index_hbm.1, f32[16,16]{1,0:T(8,128)} %coupling_hbm.1, f32[1,16,6,16,512]{4,3,2,1,0:T(8,128)} %weight_hbm.1), custom_call_target="tpu_custom_call" | custom-call | flops 200000000 | bytes 7000000 | tf_op jit(solution)/shard_map/pallas_call | solution.py:695
  45.2 1.6 %copy.8 = f32[6,16,512]{2,1,0:T(8,128)} copy(f32[6,16,512]{2,1,0:T(8,128)} %shard_map.64) | data formatting | bytes 393216
